TPU v7x, 256 devices: a whole 4x4x8 slice. The times are simulated.
256 devices in a mesh: samp: 64 (over z, y_hi, x), band: 4 (over y_lo, core).
Axes of the slice: x: 4, y: 4 (y_hi: 2, y_lo: 2; y = y_hi * 2 + y_lo), z: 8, core: 2. Of those that a mesh axis runs over, the one named last changes fastest.
Arguments:
- features: bfloat16 [16384, 1024], P('samp', 'band'), may hold values from -6 to 6
- direction: bfloat16 [16384, 256], P('samp'), may hold values from -6 to 6
- cotangent: bfloat16 [16384, 256], P('samp'), may hold values from -6 to 6
- residual: float32 [16384, 256], P('samp', 'band'), may hold values from -6 to 6
- band_logw: float32 [4], P('band'), may hold values from -1 to 1
- ridge: float32 [1], replicated, may hold values from 0.5 to 2
Outputs:
- residual_next: float32 [16384, 256], P('samp', 'band')
- adjoint: float32 [16384, 256], P('samp', 'band')
- band_grad: float32 [4], P('band')
All inputs are finite; a program needn't handle non-finite values.
Results may differ from a plain program's by a relative error of at most 0.0018.
The roundings to bfloat16 on the way count: a program that leaves them out, or rounds other values in their place, can miss the bound.
Values may be sent and summed in bfloat16 or wider, within the bound.
No kernel may reach another device: no remote copies, remote signals or barrier semaphores. Data moves between devices by JAX's collectives and lax.ppermute only.
A program may use at most 128 MiB of HBM per device.

v0:
```python
import math

import jax
import jax.numpy as jnp
from jax import lax
from jax.experimental import pallas as pl
from jax.experimental.pallas import tpu as pltpu
from jax.sharding import Mesh, PartitionSpec as P

SIZES = {"z": 8, "yh": 2, "x": 4, "yl": 2, "core": 2}
SAMP = ("z", "yh", "x")
BAND = ("yl", "core")
F32 = jnp.float32
BF16 = jnp.bfloat16
NT = (((1,), (1,)), ((), ()))
ZD = (0, 7, 1, 6, 2, 5, 3, 4)
PD = ((0, 0), (1, 0), (0, 3), (1, 3), (0, 1), (1, 1), (0, 2), (1, 2))


def send(value, axis, step):
    n = SIZES[axis]
    return lax.ppermute(value, axis, [(i, (i + step) % n) for i in range(n)])


def load_rows(xr, ct, blocks):
    for i, ref in enumerate(blocks):
        cols = slice(256 * i, 256 * i + 256)
        xr[cols, :] = ref[0:256, :]
        ct[:, cols] = ref[256:512, :]


def add_column(xr, ct, column, p_in, p_ref):
    x_c, d_c = column
    total = jnp.zeros((256, 256), F32)
    for r in range(0, 2048, 1024):
        rows = slice(r, r + 1024)
        inner = lax.dot_general(xr[rows, :], x_c, NT, preferred_element_type=F32) + 1.0
        tile = (inner * inner).astype(BF16)
        part = lax.dot_general(d_c, tile, NT, preferred_element_type=F32)
        p_ref[:, rows] = part if p_in is None else p_in[:, rows] + part
        total += jnp.dot(ct[:, rows], tile, preferred_element_type=F32)
    return total


def kernel_tiles(w_ref, pos_ref, *refs):
    z, rows = refs[0:9], refs[9:17]
    pm_ref, pq_ref, gm_ref, gq_ref, grad_ref, xr, ct, acc = refs[17:]
    w = w_ref[0]
    z_at, yh_at, x_at, yl_at = (pos_ref[i] for i in range(4))
    load_rows(xr, ct, rows)

    def emit(mine, theirs, slot, block):
        mine[2 * slot + yl_at] = block[0:64, :]
        mine[2 * slot + 1 - yl_at] = block[64:128, :]
        theirs[2 * slot + yl_at] = block[128:192, :]
        theirs[2 * slot + 1 - yl_at] = block[192:256, :]

    columns = [(ref[0:256, :], ref[256:512, :]) for ref in z[0:7]]
    columns.append((z[7][...], z[8][...]))
    for j, column in enumerate(columns):
        block = add_column(xr, ct, column, acc if j else None, acc)
        emit(gm_ref, gq_ref, lax.rem(z_at + ZD[j], 8), block * w)
    grad = jnp.zeros((256, 256), F32)
    for i, (dy, dx) in enumerate(PD):
        cols = slice(256 * i, 256 * i + 256)
        part = acc[:, cols] * w
        emit(pm_ref, pq_ref, 4 * lax.rem(yh_at + dy, 2) + lax.rem(x_at + dx, 4), part)
        grad += part * ct[:, cols].astype(F32)
    grad_ref[...] = jnp.sum(grad.reshape(32, 8, 2, 128), axis=(0, 2))


def kernel_fold(pos_ref, mine, theirs, base, grad, *refs):
    rows, out = refs[0:8], refs[21]
    yh_at, x_at, yl_at = (pos_ref[i] for i in range(1, 4))
    curve = jnp.zeros((128, 256), F32)
    for ref, (dy, dx) in zip(rows, PD):
        slot = 4 * lax.rem(yh_at + dy, 2) + lax.rem(x_at + dx, 4)
        at = (2 * slot + yl_at, 2 * slot + 1 - yl_at)
        blocks = [mine[k] + theirs[k] for k in at]
        for k, block in zip(at, blocks):
            out[k, 0:64, :] = block
        curve += jnp.concatenate(blocks) * ref[512:640, :].astype(F32)
    curve = jnp.sum((curve[:, 0:128] + curve[:, 128:256]).T, axis=0, keepdims=True)
    first = lax.broadcasted_iota(jnp.int32, (8, 128), 0) == 0
    sums = jnp.concatenate([base[...] + jnp.where(first, curve, 0.0), grad[...]], axis=1)
    for k in range(16):
        out[k, 64:72, :] = sums


def call(kernel, name, ins, outs, scratch, head=()):
    vmem = pl.BlockSpec(memory_space=pltpu.VMEM)
    return pl.pallas_call(
        kernel,
        out_shape=tuple(jax.ShapeDtypeStruct(s, F32) for s in outs),
        in_specs=[pl.BlockSpec(memory_space=pltpu.SMEM)] * len(head) + [vmem] * len(ins),
        out_specs=(vmem,) * len(outs),
        scratch_shapes=scratch,
        compiler_params=pltpu.CompilerParams(vmem_limit_bytes=16 * 1024 * 1024),
        name=name,
    )(*head, *ins)


def body(features, direction, cotangent, residual, band_logw, ridge):
    total = features.shape[0] * 64
    weight = jnp.exp(band_logw) * (1.0 / math.sqrt(total))
    yl = lax.axis_index("yl")
    core = lax.axis_index("core")

    def voxel_major(array):
        parts = [
            lax.dynamic_slice_in_dim(array, 64 * chunk, 64, 1)
            for chunk in (
                2 * yl + core,
                2 * (1 - yl) + core,
                2 * yl + 1 - core,
                2 * (1 - yl) + 1 - core,
            )
        ]
        return jnp.concatenate(parts, axis=1).T

    dir_t, cot_t = voxel_major(direction), voxel_major(cotangent)
    z0 = jnp.concatenate([features, dir_t])
    p0 = jnp.concatenate([features * jnp.bfloat16(0.0625), cot_t, dir_t[0:128]])

    f1, b1 = send(z0, "z", 1), send(z0, "z", -1)
    pf, pb = send(p0, "x", 1), send(p0, "x", -1)
    q0 = send(p0, "yh", 1)
    f1, b1, q0, pf, pb = lax.optimization_barrier((f1, b1, q0, pf, pb))
    f2, b2 = send(f1, "z", 1), send(b1, "z", -1)
    qf, qb = send(q0, "x", 1), send(q0, "x", -1)
    f2, b2, qf, qb = lax.optimization_barrier((f2, b2, qf, qb))
    f3, b3 = send(f2, "z", 1), send(b2, "z", -1)
    p2, q2 = send(pf, "x", 1), send(qb, "x", -1)
    rows = (p0, q0, pf, qf, pb, qb, p2, q2)
    f4, b4 = send(f3[0:256], "z", 1), send(b3[256:512], "z", -1)
    place = jnp.stack([lax.axis_index(a) for a in ("z", "yh", "x", "yl")]).astype(jnp.int32)
    chunks = (16, 64, 256)
    p_mine, p_other, g_mine, g_other, grad = call(
        kernel_tiles,
        "tiles",
        (z0, f1, b1, f2, b2, f3, b3, f4, b4, *rows),
        (chunks, chunks, chunks, chunks, (8, 128)),
        (
            pltpu.VMEM((2048, 256), BF16),
            pltpu.VMEM((256, 2048), BF16),
            pltpu.VMEM((256, 2048), F32),
        ),
        (weight, place),
    )

    dir_own = dir_t[0:64].astype(F32)
    res_t = residual.T
    squares = jnp.sum(res_t * res_t, axis=1)
    ridged = ridge[0] * jnp.sum(dir_own * dir_own, axis=1)
    base = jnp.pad(jnp.stack([ridged, squares]), ((0, 6), (0, 64)))
    (p_sum,) = call(
        kernel_fold,
        "fold",
        (p_mine, send(p_other, "core", 1), base, grad, *rows, z0, f1, b1, f2, b2, f3, b3, f4, b4, f1, b1, f2, b2),
        ((16, 72, 256),),
        (),
        (place,),
    )
    p_sum, g_other = lax.optimization_barrier((p_sum, g_other))
    g_sum = g_mine + send(g_other, "core", 1)
    p_all = lax.all_to_all(p_sum, ("yh", "x", "yl"), 0, 0)

    def g_block(offset):
        at = 2 * lax.rem(lax.axis_index("z") + offset, 8)
        pair = lax.dynamic_slice_in_dim(g_sum, at, 2, 0)
        return jnp.where(yl == 0, pair, pair[::-1])

    near = [send(g_block(d), "z", d) for d in (1, 7)]
    p_all, near = lax.optimization_barrier((p_all, near))
    away = [send(g_block(d), "z", d) for d in (4, 3, 5, 2, 6)]

    product = jnp.sum(p_all[:, 0:64], axis=0) + ridge[0] * dir_own
    plane = jnp.sum(p_all[:, 64:72].reshape(8, 2, 8, 256), axis=0)
    same, other = jnp.where(yl == 0, plane, plane[::-1])
    sums = jnp.concatenate(
        [same[1, 0:64], same[0, 0:64] + other[0, 64:128], jnp.sum(same[:, 128:256], axis=0)]
    )
    sums = lax.all_to_all(jnp.broadcast_to(sums.reshape(1, 1, 256), (8, 1, 256)), "z", 0, 0)
    sums, away = lax.optimization_barrier((sums, away))
    sums = jnp.sum(sums, axis=0)
    adj = g_block(0) + sum(near + away)
    adj = adj[0] + send(adj[1], "yl", 1)
    adjoint = adj + ridge[0] * cot_t[0:64].astype(F32)
    ratio = sums[0, 0:64] / sums[0, 64:128]
    residual_next = res_t - ratio[:, None] * product
    return (residual_next.T, adjoint.T, jnp.sum(sums[0, 128:256]).reshape(1))


def solution(mesh):
    parts = Mesh(mesh.devices.reshape(tuple(SIZES.values())), tuple(SIZES))
    placed = (P(SAMP, BAND), P(SAMP), P(SAMP), P(SAMP, BAND), P(BAND), P())
    return jax.shard_map(
        body,
        mesh=parts,
        in_specs=placed,
        out_specs=(P(SAMP, BAND), P(SAMP, BAND), P(BAND)),
        check_vma=False,
    )
```

profile of v0, /device:TPU:2, one launch (start us, length us, event | category | flops | bytes accessed | tf_op | source)
XLA Modules:
  0.0 108.7 jit_solution(9498429955019140500)
XLA Ops:
  0.7 1.3 %constant_dynamic-slice_fusion.11 = (bf16[256,64]{1,0:T(8,128)(2,1)S(1)}, bf16[256,64]{1,0:T(8,128)(2,1)S(1)}, bf16[256,64]{1,0:T(8,128)(2,1)S(1)}, bf16[256,64]...) fusion(bf16[256,256]{1,0:T(8,128)(2,1)} %param.8, ...), kind=kLoop, calls=%fused_computation.47 | loop fusion | bytes 524304 | tf_op jit(solution)/shard_map/dynamic_slice | solution.py:111
  2.9 3.3 %collective-permute-start.2 = (bf16[640,256]{1,0:T(8,128)(2,1)S(1)}, bf16[640,256]{1,0:T(8,128)(2,1)S(1)}, u32[]{:S(2)}, u32[]{:S(2)}) collective-permute-start(bf16[640,256]{1,0:T(8,128)(2,1)S(1)} %pad_maximum_fusion.refs_9_.refs_0_), channel_id=1, source_target_pairs={{0,16},{16,0},{1,17},{17,1},{2,18},{18,2},{3,19},{19,3},{4,20},{20... | collective-permute-start | bytes 983048 | tf_op jit(solution)/shard_map/ppermute | solution.py:22
  6.2 1.5 %collective-permute-start.3 = (bf16[640,256]{1,0:T(8,128)(2,1)S(1)}, bf16[640,256]{1,0:T(8,128)(2,1)S(1)}, u32[]{:S(2)}, u32[]{:S(2)}) collective-permute-start(bf16[640,256]{1,0:T(8,128)(2,1)S(1)} %pad_maximum_fusion.refs_9_.refs_0_), channel_id=1, source_target_pairs={{0,4},{4,8},{8,12},{12,0},{1,5},{5,9},{9,13},{13,1},{2,6},{6,10},{... | collective-permute-start | bytes 983048 | tf_op jit(solution)/shard_map/ppermute | solution.py:22
  8.2 2.0 %collective-permute-start = (bf16[512,256]{1,0:T(8,128)(2,1)S(1)}, bf16[512,256]{1,0:T(8,128)(2,1)S(1)}, u32[]{:S(2)}, u32[]{:S(2)}) collective-permute-start(bf16[512,256]{1,0:T(8,128)(2,1)S(1)} %pad_maximum_fusion.1.refs_0_.refs_8_), channel_id=1, source_target_pairs={{0,32},{32,64},{64,96},{96,128},{128,160},{160,192},{192,224},{224... | collective-permute-start | bytes 786440 | tf_op jit(solution)/shard_map/ppermute | solution.py:22
  10.2 4.0 %collective-permute-start.1 = (bf16[512,256]{1,0:T(8,128)(2,1)S(1)}, bf16[512,256]{1,0:T(8,128)(2,1)S(1)}, u32[]{:S(2)}, u32[]{:S(2)}) collective-permute-start(bf16[512,256]{1,0:T(8,128)(2,1)S(1)} %pad_maximum_fusion.1.refs_0_.refs_8_), channel_id=1, source_target_pairs={{0,224},{32,0},{64,32},{96,64},{128,96},{160,128},{192,160},{224,1... | collective-permute-start | bytes 786440 | tf_op jit(solution)/shard_map/ppermute | solution.py:22
  14.2 5.4 %collective-permute-done.refs_1_.refs_9_.refs_17_ = bf16[512,256]{1,0:T(8,128)(2,1)S(1)} collective-permute-done((bf16[512,256]{1,0:T(8,128)(2,1)S(1)}, bf16[512,256]{1,0:T(8,128)(2,1)S(1)}, u32[]{:S(2)}, u32[]{:S(2)}) %collective-permute-start) | collective-permute-done | bytes 262176 | tf_op jit(solution)/shard_map/ppermute | solution.py:22
  19.6 1.6 %collective-permute-start.7 = (bf16[640,256]{1,0:T(8,128)(2,1)S(1)}, bf16[640,256]{1,0:T(8,128)(2,1)S(1)}, u32[]{:S(2)}, u32[]{:S(2)}) collective-permute-start(bf16[640,256]{1,0:T(8,128)(2,1)S(1)} %collective-permute-done.2.refs_10_.refs_1_), channel_id=1, source_target_pairs={{0,4},{4,8},{8,12},{12,0},{1,5},{5,9},{9,13},{13,1},{2,6},{6,10},{... | collective-permute-start | bytes 983048 | tf_op jit(solution)/shard_map/ppermute | solution.py:22
  21.8 3.2 %collective-permute-start.6 = (bf16[512,256]{1,0:T(8,128)(2,1)S(1)}, bf16[512,256]{1,0:T(8,128)(2,1)S(1)}, u32[]{:S(2)}, u32[]{:S(2)}) collective-permute-start(bf16[512,256]{1,0:T(8,128)(2,1)S(1)} %collective-permute-done.1.refs_2_.refs_10_.refs_18_), channel_id=1, source_target_pairs={{0,224},{32,0},{64,32},{96,64},{128,96},{160,128},{192,160},{224,1... | collective-permute-start | bytes 786440 | tf_op jit(solution)/shard_map/ppermute | solution.py:22
  25.0 4.3 %collective-permute-done.5.refs_3_.refs_11_.refs_19_ = bf16[512,256]{1,0:T(8,128)(2,1)S(1)} collective-permute-done((bf16[512,256]{1,0:T(8,128)(2,1)S(1)}, bf16[512,256]{1,0:T(8,128)(2,1)S(1)}, u32[]{:S(2)}, u32[]{:S(2)}) %collective-permute-start.5) | collective-permute-done | bytes 262176 | tf_op jit(solution)/shard_map/ppermute | solution.py:22
  29.3 2.4 %collective-permute-start.9 = (bf16[512,256]{1,0:T(8,128)(2,1)S(1)}, bf16[512,256]{1,0:T(8,128)(2,1)S(1)}, u32[]{:S(2)}, u32[]{:S(2)}) collective-permute-start(bf16[512,256]{1,0:T(8,128)(2,1)S(1)} %collective-permute-done.5.refs_3_.refs_11_.refs_19_), channel_id=1, source_target_pairs={{0,32},{32,64},{64,96},{96,128},{128,160},{160,192},{192,224},{224... | collective-permute-start | bytes 786440 | tf_op jit(solution)/shard_map/ppermute | solution.py:22
  32.7 1.5 %collective-permute-start.13 = (bf16[640,256]{1,0:T(8,128)(2,1)S(1)}, bf16[640,256]{1,0:T(8,128)(2,1)}, u32[]{:S(2)}, u32[]{:S(2)}) collective-permute-start(bf16[640,256]{1,0:T(8,128)(2,1)S(1)} %collective-permute-done.3.refs_11_.refs_2_), channel_id=1, source_target_pairs={{0,4},{4,8},{8,12},{12,0},{1,5},{5,9},{9,13},{13,1},{2,6},{6,10},{... | collective-permute-start | bytes 983048 | tf_op jit(solution)/shard_map/ppermute | solution.py:22
  34.2 1.5 %collective-permute-start.14 = (bf16[640,256]{1,0:T(8,128)(2,1)}, bf16[640,256]{1,0:T(8,128)(2,1)}, u32[]{:S(2)}, u32[]{:S(2)}) collective-permute-start(bf16[640,256]{1,0:T(8,128)(2,1)} %collective-permute-done.8.refs_14_.refs_5_), channel_id=1, source_target_pairs={{0,12},{4,0},{8,4},{12,8},{1,13},{5,1},{9,5},{13,9},{2,14},{6,2},{... | collective-permute-start | bytes 983048 | tf_op jit(solution)/shard_map/ppermute | solution.py:22
  35.6 1.4 %collective-permute-done.9.refs_5_.refs_13_ = bf16[512,256]{1,0:T(8,128)(2,1)S(1)} collective-permute-done((bf16[512,256]{1,0:T(8,128)(2,1)S(1)}, bf16[512,256]{1,0:T(8,128)(2,1)S(1)}, u32[]{:S(2)}, u32[]{:S(2)}) %collective-permute-start.9) | collective-permute-done | bytes 262176 | tf_op jit(solution)/shard_map/ppermute | solution.py:22
  37.7 2.2 %collective-permute-start.11 = (bf16[256,256]{1,0:T(8,128)(2,1)}, bf16[256,256]{1,0:T(8,128)(2,1)}, u32[]{:S(2)}, u32[]{:S(2)}) collective-permute-start(bf16[256,256]{1,0:T(8,128)(2,1)} %slice.65), channel_id=1, source_target_pairs={{0,32},{32,64},{64,96},{96,128},{128,160},{160,192},{192,224},{224... | collective-permute-start | bytes 393224 | tf_op jit(solution)/shard_map/ppermute | solution.py:22
  40.5 1.0 collective-permute-start.12
  42.3 1.8 %collective-permute-done.11.refs_7_.refs_15_ = bf16[256,256]{1,0:T(8,128)(2,1)} collective-permute-done((bf16[256,256]{1,0:T(8,128)(2,1)}, bf16[256,256]{1,0:T(8,128)(2,1)}, u32[]{:S(2)}, u32[]{:S(2)}) %collective-permute-start.11) | collective-permute-done | bytes 131104 | tf_op jit(solution)/shard_map/ppermute | solution.py:22
  44.2 1.9 %collective-permute-done.12.refs_8_.refs_16_ = bf16[256,256]{1,0:T(8,128)(2,1)} collective-permute-done((bf16[256,256]{1,0:T(8,128)(2,1)}, bf16[256,256]{1,0:T(8,128)(2,1)}, u32[]{:S(2)}, u32[]{:S(2)}) %collective-permute-start.12) | collective-permute-done | bytes 131104 | tf_op jit(solution)/shard_map/ppermute | solution.py:22
  46.1 9.1 %tiles.1 = (f32[16,64,256]{2,1,0:T(8,128)S(1)}, f32[16,64,256]{2,1,0:T(8,128)S(1)}, f32[16,64,256]{2,1,0:T(8,128)S(1)}, f32[16,64,256]{2,1,0:T(8,128)}, f32[8,128]{1,0:T(8,128)S(1)}) custom-call(f32[1]{0:T(128)S(6)} %mul.101.w_ref, s32[4]{0:T(128)S(1)} %pad_add_fusion.pos_ref, bf16[512,256]{1,0:T(8,128)(2,1)S(1)} %pad_maximum_fusion.1.refs_0_.refs_8_, ...), custom_call_target="tpu_custom_call" | custom-call | tf_op jit(solution)/shard_map/tiles/pallas_call | solution.py:92
  55.2 1.0 copy-done
  58.9 2.7 %fold.1 = f32[16,72,256]{2,1,0:T(8,128)} custom-call(s32[4]{0:T(128)S(1)} %pad_add_fusion.pos_ref, f32[16,64,256]{2,1,0:T(8,128)S(1)} %get-tuple-element.37.mine, f32[16,64,256]{2,1,0:T(8,128)S(1)} %collective-permute-done.15.theirs, f32[8,128]{1,0:T(8,128)S(1)} %select_maximum_fusion.base, f32[8,128]{1,0:T(8,128)S(1)} %get-tuple-element.39.grad, ...), custom_call_target="tpu_custom_call" | custom-call | tf_op jit(solution)/shard_map/fold/pallas_call | solution.py:92
  61.7 6.7 %all-to-all-start = ((f32[16,72,256]{2,1,0:T(8,128)}), f32[16,72,256]{2,1,0:T(8,128)S(1)}, u32[]{:S(2)}, u32[]{:S(2)}) async-start(f32[16,72,256]{2,1,0:T(8,128)} %fold.1), calls=%async_computation | async-start | bytes 2359296 | tf_op jit(solution)/shard_map/all_to_all | solution.py:166
  68.7 2.0 %collective-permute-start.18 = (f32[2,64,256]{2,1,0:T(8,128)S(1)}, f32[2,64,256]{2,1,0:T(8,128)S(1)}, u32[]{:S(2)}, u32[]{:S(2)}) collective-permute-start(f32[2,64,256]{2,1,0:T(8,128)S(1)} %reverse_select_fusion.6), channel_id=1, source_target_pairs={{0,224},{32,0},{64,32},{96,64},{128,96},{160,128},{192,160},{224,1... | collective-permute-start | bytes 393224 | tf_op jit(solution)/shard_map/ppermute | solution.py:22
  70.9 4.2 %collective-permute-start.19 = (f32[2,64,256]{2,1,0:T(8,128)S(1)}, f32[2,64,256]{2,1,0:T(8,128)S(1)}, u32[]{:S(2)}, u32[]{:S(2)}) collective-permute-start(f32[2,64,256]{2,1,0:T(8,128)S(1)} %reverse_select_fusion.5), channel_id=1, source_target_pairs={{0,128},{32,160},{64,192},{96,224},{128,0},{160,32},{192,64},{224,... | collective-permute-start | bytes 393224 | tf_op jit(solution)/shard_map/ppermute | solution.py:22
  75.2 2.3 %collective-permute-start.20 = (f32[2,64,256]{2,1,0:T(8,128)S(1)}, f32[2,64,256]{2,1,0:T(8,128)S(1)}, u32[]{:S(2)}, u32[]{:S(2)}) collective-permute-start(f32[2,64,256]{2,1,0:T(8,128)S(1)} %reverse_select_fusion.4), channel_id=1, source_target_pairs={{0,96},{32,128},{64,160},{96,192},{128,224},{160,0},{192,32},{224,... | collective-permute-start | bytes 393224 | tf_op jit(solution)/shard_map/ppermute | solution.py:22
  77.5 3.1 %collective-permute-start.21 = (f32[2,64,256]{2,1,0:T(8,128)S(1)}, f32[2,64,256]{2,1,0:T(8,128)S(1)}, u32[]{:S(2)}, u32[]{:S(2)}) collective-permute-start(f32[2,64,256]{2,1,0:T(8,128)S(1)} %reverse_select_fusion.3), channel_id=1, source_target_pairs={{0,160},{32,192},{64,224},{96,0},{128,32},{160,64},{192,96},{224,1... | collective-permute-start | bytes 393224 | tf_op jit(solution)/shard_map/ppermute | solution.py:22
  81.3 3.6 %collective-permute-start.23 = (f32[2,64,256]{2,1,0:T(8,128)S(1)}, f32[2,64,256]{2,1,0:T(8,128)S(1)}, u32[]{:S(2)}, u32[]{:S(2)}) collective-permute-start(f32[2,64,256]{2,1,0:T(8,128)S(1)} %reverse_select_fusion.1), channel_id=1, source_target_pairs={{0,192},{32,224},{64,0},{96,32},{128,64},{160,96},{192,128},{224,1... | collective-permute-start | bytes 393224 | tf_op jit(solution)/shard_map/ppermute | solution.py:22
  85.7 9.4 %all-to-all-start.1 = ((f32[8,1,256]{2,1,0:T(1,128)}), f32[8,1,256]{2,1,0:T(1,128)S(1)}, u32[]{:S(2)}, u32[]{:S(2)}) async-start(f32[8,1,256]{2,1,0:T(1,128)} %broadcast_in_dim.2), calls=%async_computation.1 | async-start | bytes 16384 | tf_op jit(solution)/shard_map/all_to_all | solution.py:183
  95.2 1.4 %collective-permute-done.22 = f32[2,64,256]{2,1,0:T(8,128)S(1)} collective-permute-done((f32[2,64,256]{2,1,0:T(8,128)S(1)}, f32[2,64,256]{2,1,0:T(8,128)S(1)}, u32[]{:S(2)}, u32[]{:S(2)}) %collective-permute-start.22) | collective-permute-done | bytes 131104 | tf_op jit(solution)/shard_map/ppermute | solution.py:22
  97.2 5.6 %all-to-all-done.1 = f32[8,1,256]{2,1,0:T(1,128)S(1)} async-done(((f32[8,1,256]{2,1,0:T(1,128)}), f32[8,1,256]{2,1,0:T(1,128)S(1)}, u32[]{:S(2)}, u32[]{:S(2)}) %all-to-all-start.1) | async-done | bytes 8224 | tf_op jit(solution)/shard_map/all_to_all | solution.py:183
  102.9 1.6 %collective-permute-start.24 = (f32[64,256]{1,0:T(8,128)S(1)}, f32[64,256]{1,0:T(8,128)S(1)}, u32[]{:S(2)}, u32[]{:S(2)}) collective-permute-start(f32[64,256]{1,0:T(8,128)S(1)} %slice_bitcast_fusion), channel_id=1, source_target_pairs={{0,2},{2,0},{1,3},{3,1},{4,6},{6,4},{5,7},{7,5},{8,10},{10,8},{9,1... | collective-permute-start | bytes 196616 | tf_op jit(solution)/shard_map/ppermute | solution.py:22
  104.6 1.5 %fusion.5 = f32[256,64]{0,1:T(8,128)} fusion(f32[64,256]{1,0:T(8,128)S(1)} %slice_reduce_fusion, f32[256,64]{0,1:T(8,128)S(1)} %copy-done.5, f32[]{:T(128)} %bitcast.45, f32[64]{0:T(128)S(1)} %fusion.11, bf16[256,256]{1,0:T(8,128)(2,1)} %copy-done.2), kind=kLoop, calls=%fused_computation.20 | loop fusion | flops 81920 | bytes 229636 | tf_op jit(solution)/shard_map/transpose | solution.py:191
  107.3 1.4 %fusion.8 = f32[256,64]{0,1:T(8,128)} fusion(f32[64,256]{1,0:T(8,128)S(1)} %collective-permute-done.24, f32[2,64,256]{2,1,0:T(8,128)S(1)} %fusion, bf16[256,256]{1,0:T(8,128)(2,1)} %copy-done.3, f32[]{:T(128)} %bitcast.46), kind=kLoop, calls=%fused_computation.25 | loop fusion | flops 65536 | bytes 229380 | tf_op jit(solution)/shard_map/transpose | solution.py:191
  (83 shorter events, 10.4 us)
Async XLA Ops:
  0.6 2.2 %copy-start.4 = (bf16[256,256]{1,0:T(8,128)(2,1)S(1)}, bf16[256,256]{1,0:T(8,128)(2,1)}, u32[]{:S(2)}) copy-start(bf16[256,256]{1,0:T(8,128)(2,1)} %param.6) | copy-start | bytes 393220
  2.8 5.4 %copy-start.2 = (bf16[256,256]{1,0:T(8,128)(2,1)}, bf16[256,256]{1,0:T(8,128)(2,1)S(1)}, u32[]{:S(2)}) copy-start(bf16[256,256]{1,0:T(8,128)(2,1)S(1)} %maximum_bitcast_fusion) | copy-start | bytes 393220
  2.8 4.8 %copy-start.3 = (bf16[256,256]{1,0:T(8,128)(2,1)}, bf16[256,256]{1,0:T(8,128)(2,1)S(1)}, u32[]{:S(2)}) copy-start(bf16[256,256]{1,0:T(8,128)(2,1)S(1)} %maximum_bitcast_fusion.1) | copy-start | bytes 393220
  2.9 16.7 %collective-permute-start.2 = (bf16[640,256]{1,0:T(8,128)(2,1)S(1)}, bf16[640,256]{1,0:T(8,128)(2,1)S(1)}, u32[]{:S(2)}, u32[]{:S(2)}) collective-permute-start(bf16[640,256]{1,0:T(8,128)(2,1)S(1)} %pad_maximum_fusion.refs_9_.refs_0_), channel_id=1, source_target_pairs={{0,16},{16,0},{1,17},{17,1},{2,18},{18,2},{3,19},{19,3},{4,20},{20... | collective-permute-start | bytes 983048 | tf_op jit(solution)/shard_map/ppermute | solution.py:22
  6.2 13.5 %collective-permute-start.3 = (bf16[640,256]{1,0:T(8,128)(2,1)S(1)}, bf16[640,256]{1,0:T(8,128)(2,1)S(1)}, u32[]{:S(2)}, u32[]{:S(2)}) collective-permute-start(bf16[640,256]{1,0:T(8,128)(2,1)S(1)} %pad_maximum_fusion.refs_9_.refs_0_), channel_id=1, source_target_pairs={{0,4},{4,8},{8,12},{12,0},{1,5},{5,9},{9,13},{13,1},{2,6},{6,10},{... | collective-permute-start | bytes 983048 | tf_op jit(solution)/shard_map/ppermute | solution.py:22
  7.7 12.0 %collective-permute-start.4 = (bf16[640,256]{1,0:T(8,128)(2,1)S(1)}, bf16[640,256]{1,0:T(8,128)(2,1)S(1)}, u32[]{:S(2)}, u32[]{:S(2)}) collective-permute-start(bf16[640,256]{1,0:T(8,128)(2,1)S(1)} %pad_maximum_fusion.refs_9_.refs_0_), channel_id=1, source_target_pairs={{0,12},{4,0},{8,4},{12,8},{1,13},{5,1},{9,5},{13,9},{2,14},{6,2},{... | collective-permute-start | bytes 983048 | tf_op jit(solution)/shard_map/ppermute | solution.py:22
  8.2 11.4 %collective-permute-start = (bf16[512,256]{1,0:T(8,128)(2,1)S(1)}, bf16[512,256]{1,0:T(8,128)(2,1)S(1)}, u32[]{:S(2)}, u32[]{:S(2)}) collective-permute-start(bf16[512,256]{1,0:T(8,128)(2,1)S(1)} %pad_maximum_fusion.1.refs_0_.refs_8_), channel_id=1, source_target_pairs={{0,32},{32,64},{64,96},{96,128},{128,160},{160,192},{192,224},{224... | collective-permute-start | bytes 786440 | tf_op jit(solution)/shard_map/ppermute | solution.py:22
  10.2 9.4 %collective-permute-start.1 = (bf16[512,256]{1,0:T(8,128)(2,1)S(1)}, bf16[512,256]{1,0:T(8,128)(2,1)S(1)}, u32[]{:S(2)}, u32[]{:S(2)}) collective-permute-start(bf16[512,256]{1,0:T(8,128)(2,1)S(1)} %pad_maximum_fusion.1.refs_0_.refs_8_), channel_id=1, source_target_pairs={{0,224},{32,0},{64,32},{96,64},{128,96},{160,128},{192,160},{224,1... | collective-permute-start | bytes 786440 | tf_op jit(solution)/shard_map/ppermute | solution.py:22
  19.6 9.7 %collective-permute-start.7 = (bf16[640,256]{1,0:T(8,128)(2,1)S(1)}, bf16[640,256]{1,0:T(8,128)(2,1)S(1)}, u32[]{:S(2)}, u32[]{:S(2)}) collective-permute-start(bf16[640,256]{1,0:T(8,128)(2,1)S(1)} %collective-permute-done.2.refs_10_.refs_1_), channel_id=1, source_target_pairs={{0,4},{4,8},{8,12},{12,0},{1,5},{5,9},{9,13},{13,1},{2,6},{6,10},{... | collective-permute-start | bytes 983048 | tf_op jit(solution)/shard_map/ppermute | solution.py:22
  21.2 8.1 %collective-permute-start.8 = (bf16[640,256]{1,0:T(8,128)(2,1)S(1)}, bf16[640,256]{1,0:T(8,128)(2,1)}, u32[]{:S(2)}, u32[]{:S(2)}) collective-permute-start(bf16[640,256]{1,0:T(8,128)(2,1)S(1)} %collective-permute-done.2.refs_10_.refs_1_), channel_id=1, source_target_pairs={{0,12},{4,0},{8,4},{12,8},{1,13},{5,1},{9,5},{13,9},{2,14},{6,2},{... | collective-permute-start | bytes 983048 | tf_op jit(solution)/shard_map/ppermute | solution.py:22
  21.7 7.6 %collective-permute-start.5 = (bf16[512,256]{1,0:T(8,128)(2,1)S(1)}, bf16[512,256]{1,0:T(8,128)(2,1)S(1)}, u32[]{:S(2)}, u32[]{:S(2)}) collective-permute-start(bf16[512,256]{1,0:T(8,128)(2,1)S(1)} %collective-permute-done.refs_1_.refs_9_.refs_17_), channel_id=1, source_target_pairs={{0,32},{32,64},{64,96},{96,128},{128,160},{160,192},{192,224},{224... | collective-permute-start | bytes 786440 | tf_op jit(solution)/shard_map/ppermute | solution.py:22
  21.8 7.6 %collective-permute-start.6 = (bf16[512,256]{1,0:T(8,128)(2,1)S(1)}, bf16[512,256]{1,0:T(8,128)(2,1)S(1)}, u32[]{:S(2)}, u32[]{:S(2)}) collective-permute-start(bf16[512,256]{1,0:T(8,128)(2,1)S(1)} %collective-permute-done.1.refs_2_.refs_10_.refs_18_), channel_id=1, source_target_pairs={{0,224},{32,0},{64,32},{96,64},{128,96},{160,128},{192,160},{224,1... | collective-permute-start | bytes 786440 | tf_op jit(solution)/shard_map/ppermute | solution.py:22
  29.3 7.7 %collective-permute-start.9 = (bf16[512,256]{1,0:T(8,128)(2,1)S(1)}, bf16[512,256]{1,0:T(8,128)(2,1)S(1)}, u32[]{:S(2)}, u32[]{:S(2)}) collective-permute-start(bf16[512,256]{1,0:T(8,128)(2,1)S(1)} %collective-permute-done.5.refs_3_.refs_11_.refs_19_), channel_id=1, source_target_pairs={{0,32},{32,64},{64,96},{96,128},{128,160},{160,192},{192,224},{224... | collective-permute-start | bytes 786440 | tf_op jit(solution)/shard_map/ppermute | solution.py:22
  31.8 8.1 %collective-permute-start.10 = (bf16[512,256]{1,0:T(8,128)(2,1)S(1)}, bf16[512,256]{1,0:T(8,128)(2,1)S(1)}, u32[]{:S(2)}, u32[]{:S(2)}) collective-permute-start(bf16[512,256]{1,0:T(8,128)(2,1)S(1)} %collective-permute-done.6.refs_4_.refs_12_.refs_20_), channel_id=1, source_target_pairs={{0,224},{32,0},{64,32},{96,64},{128,96},{160,128},{192,160},{224,1... | collective-permute-start | bytes 786440 | tf_op jit(solution)/shard_map/ppermute | solution.py:22
  32.7 9.7 %collective-permute-start.13 = (bf16[640,256]{1,0:T(8,128)(2,1)S(1)}, bf16[640,256]{1,0:T(8,128)(2,1)}, u32[]{:S(2)}, u32[]{:S(2)}) collective-permute-start(bf16[640,256]{1,0:T(8,128)(2,1)S(1)} %collective-permute-done.3.refs_11_.refs_2_), channel_id=1, source_target_pairs={{0,4},{4,8},{8,12},{12,0},{1,5},{5,9},{9,13},{13,1},{2,6},{6,10},{... | collective-permute-start | bytes 983048 | tf_op jit(solution)/shard_map/ppermute | solution.py:22
  34.2 8.2 %collective-permute-start.14 = (bf16[640,256]{1,0:T(8,128)(2,1)}, bf16[640,256]{1,0:T(8,128)(2,1)}, u32[]{:S(2)}, u32[]{:S(2)}) collective-permute-start(bf16[640,256]{1,0:T(8,128)(2,1)} %collective-permute-done.8.refs_14_.refs_5_), channel_id=1, source_target_pairs={{0,12},{4,0},{8,4},{12,8},{1,13},{5,1},{9,5},{13,9},{2,14},{6,2},{... | collective-permute-start | bytes 983048 | tf_op jit(solution)/shard_map/ppermute | solution.py:22
  37.7 6.5 %collective-permute-start.11 = (bf16[256,256]{1,0:T(8,128)(2,1)}, bf16[256,256]{1,0:T(8,128)(2,1)}, u32[]{:S(2)}, u32[]{:S(2)}) collective-permute-start(bf16[256,256]{1,0:T(8,128)(2,1)} %slice.65), channel_id=1, source_target_pairs={{0,32},{32,64},{64,96},{96,128},{128,160},{160,192},{192,224},{224... | collective-permute-start | bytes 393224 | tf_op jit(solution)/shard_map/ppermute | solution.py:22
  40.5 5.6 %collective-permute-start.12 = (bf16[256,256]{1,0:T(8,128)(2,1)}, bf16[256,256]{1,0:T(8,128)(2,1)}, u32[]{:S(2)}, u32[]{:S(2)}) collective-permute-start(bf16[256,256]{1,0:T(8,128)(2,1)} %slice.66), channel_id=1, source_target_pairs={{0,224},{32,0},{64,32},{96,64},{128,96},{160,128},{192,160},{224,1... | collective-permute-start | bytes 393224 | tf_op jit(solution)/shard_map/ppermute | solution.py:22
  42.3 15.4 %copy-start.5 = (f32[256,64]{0,1:T(8,128)S(1)}, f32[256,64]{0,1:T(8,128)}, u32[]{:S(2)}) copy-start(f32[256,64]{0,1:T(8,128)} %param.9) | copy-start | bytes 196612
  56.2 2.7 %collective-permute-start.15 = (f32[16,64,256]{2,1,0:T(8,128)S(1)}, f32[16,64,256]{2,1,0:T(8,128)S(1)}, u32[]{:S(2)}, u32[]{:S(2)}) collective-permute-start(f32[16,64,256]{2,1,0:T(8,128)S(1)} %get-tuple-element.38), channel_id=1, source_target_pairs={{0,1},{1,0},{2,3},{3,2},{4,5},{5,4},{6,7},{7,6},{8,9},{9,8},{10,11... | collective-permute-start | bytes 3145736 | tf_op jit(solution)/shard_map/ppermute | solution.py:22
  61.6 6.8 %collective-permute-start.16 = (f32[16,64,256]{2,1,0:T(8,128)}, f32[16,64,256]{2,1,0:T(8,128)S(1)}, u32[]{:S(2)}, u32[]{:S(2)}) collective-permute-start(f32[16,64,256]{2,1,0:T(8,128)} %get-tuple-element.43), channel_id=1, source_target_pairs={{0,1},{1,0},{2,3},{3,2},{4,5},{5,4},{6,7},{7,6},{8,9},{9,8},{10,11... | collective-permute-start | bytes 3145736 | tf_op jit(solution)/shard_map/ppermute | solution.py:22
  61.7 6.7 %copy-start.1 = (f32[16,64,256]{2,1,0:T(8,128)S(1)}, f32[16,64,256]{2,1,0:T(8,128)}, u32[]{:S(2)}) copy-start(f32[16,64,256]{2,1,0:T(8,128)} %copy-done) | copy-start | bytes 3145732
  61.7 23.2 %all-to-all-start = ((f32[16,72,256]{2,1,0:T(8,128)}), f32[16,72,256]{2,1,0:T(8,128)S(1)}, u32[]{:S(2)}, u32[]{:S(2)}) async-start(f32[16,72,256]{2,1,0:T(8,128)} %fold.1), calls=%async_computation | async-start | bytes 2359296 | tf_op jit(solution)/shard_map/all_to_all | solution.py:166
  68.7 11.9 %collective-permute-start.18 = (f32[2,64,256]{2,1,0:T(8,128)S(1)}, f32[2,64,256]{2,1,0:T(8,128)S(1)}, u32[]{:S(2)}, u32[]{:S(2)}) collective-permute-start(f32[2,64,256]{2,1,0:T(8,128)S(1)} %reverse_select_fusion.6), channel_id=1, source_target_pairs={{0,224},{32,0},{64,32},{96,64},{128,96},{160,128},{192,160},{224,1... | collective-permute-start | bytes 393224 | tf_op jit(solution)/shard_map/ppermute | solution.py:22
  70.7 10.6 %collective-permute-start.17 = (f32[2,64,256]{2,1,0:T(8,128)S(1)}, f32[2,64,256]{2,1,0:T(8,128)S(1)}, u32[]{:S(2)}, u32[]{:S(2)}) collective-permute-start(f32[2,64,256]{2,1,0:T(8,128)S(1)} %reverse_select_fusion.7), channel_id=1, source_target_pairs={{0,32},{32,64},{64,96},{96,128},{128,160},{160,192},{192,224},{224... | collective-permute-start | bytes 393224 | tf_op jit(solution)/shard_map/ppermute | solution.py:22
  70.9 24.2 %collective-permute-start.19 = (f32[2,64,256]{2,1,0:T(8,128)S(1)}, f32[2,64,256]{2,1,0:T(8,128)S(1)}, u32[]{:S(2)}, u32[]{:S(2)}) collective-permute-start(f32[2,64,256]{2,1,0:T(8,128)S(1)} %reverse_select_fusion.5), channel_id=1, source_target_pairs={{0,128},{32,160},{64,192},{96,224},{128,0},{160,32},{192,64},{224,... | collective-permute-start | bytes 393224 | tf_op jit(solution)/shard_map/ppermute | solution.py:22
  75.2 20.0 %collective-permute-start.20 = (f32[2,64,256]{2,1,0:T(8,128)S(1)}, f32[2,64,256]{2,1,0:T(8,128)S(1)}, u32[]{:S(2)}, u32[]{:S(2)}) collective-permute-start(f32[2,64,256]{2,1,0:T(8,128)S(1)} %reverse_select_fusion.4), channel_id=1, source_target_pairs={{0,96},{32,128},{64,160},{96,192},{128,224},{160,0},{192,32},{224,... | collective-permute-start | bytes 393224 | tf_op jit(solution)/shard_map/ppermute | solution.py:22
  77.5 17.7 %collective-permute-start.21 = (f32[2,64,256]{2,1,0:T(8,128)S(1)}, f32[2,64,256]{2,1,0:T(8,128)S(1)}, u32[]{:S(2)}, u32[]{:S(2)}) collective-permute-start(f32[2,64,256]{2,1,0:T(8,128)S(1)} %reverse_select_fusion.3), channel_id=1, source_target_pairs={{0,160},{32,192},{64,224},{96,0},{128,32},{160,64},{192,96},{224,1... | collective-permute-start | bytes 393224 | tf_op jit(solution)/shard_map/ppermute | solution.py:22
  80.7 15.9 %collective-permute-start.22 = (f32[2,64,256]{2,1,0:T(8,128)S(1)}, f32[2,64,256]{2,1,0:T(8,128)S(1)}, u32[]{:S(2)}, u32[]{:S(2)}) collective-permute-start(f32[2,64,256]{2,1,0:T(8,128)S(1)} %reverse_select_fusion.2), channel_id=1, source_target_pairs={{0,64},{32,96},{64,128},{96,160},{128,192},{160,224},{192,0},{224,... | collective-permute-start | bytes 393224 | tf_op jit(solution)/shard_map/ppermute | solution.py:22
  81.3 15.9 %collective-permute-start.23 = (f32[2,64,256]{2,1,0:T(8,128)S(1)}, f32[2,64,256]{2,1,0:T(8,128)S(1)}, u32[]{:S(2)}, u32[]{:S(2)}) collective-permute-start(f32[2,64,256]{2,1,0:T(8,128)S(1)} %reverse_select_fusion.1), channel_id=1, source_target_pairs={{0,192},{32,224},{64,0},{96,32},{128,64},{160,96},{192,128},{224,1... | collective-permute-start | bytes 393224 | tf_op jit(solution)/shard_map/ppermute | solution.py:22
  85.7 17.1 %all-to-all-start.1 = ((f32[8,1,256]{2,1,0:T(1,128)}), f32[8,1,256]{2,1,0:T(1,128)S(1)}, u32[]{:S(2)}, u32[]{:S(2)}) async-start(f32[8,1,256]{2,1,0:T(1,128)} %broadcast_in_dim.2), calls=%async_computation.1 | async-start | bytes 16384 | tf_op jit(solution)/shard_map/all_to_all | solution.py:183
  102.9 4.4 %collective-permute-start.24 = (f32[64,256]{1,0:T(8,128)S(1)}, f32[64,256]{1,0:T(8,128)S(1)}, u32[]{:S(2)}, u32[]{:S(2)}) collective-permute-start(f32[64,256]{1,0:T(8,128)S(1)} %slice_bitcast_fusion), channel_id=1, source_target_pairs={{0,2},{2,0},{1,3},{3,1},{4,6},{6,4},{5,7},{7,5},{8,10},{10,8},{9,1... | collective-permute-start | bytes 196616 | tf_op jit(solution)/shard_map/ppermute | solution.py:22
  (1 other events, 1.0 us)
where the time goes:
time: 109 us
  starting transfers between devices  59.9 us (55%)
  waiting for transfers between devices  24.2 us (22%)
  Pallas kernels  11.8 us (11%)
  other arithmetic  5.27 us (5%)
  local copies, waits for them, and re-layouts  5.11 us (5%)
  between operations  2.34 us (2%)
    ppermute x25, starting transfers between devices, send(): return lax.ppermute(value, axis, [(i, (i + step) % n) for i in range(n)])  43.9 us
    ppermute x25, waiting for transfers between devices, send(): return lax.ppermute(value, axis, [(i, (i + step) % n) for i in range(n)])  18.5 us
    pallas_call x2, Pallas kernels, call(): pl.pallas_call(kernel, out_shape=tuple((jax.ShapeDtypeStruct(s, F32) for...  11.8 us
    all_to_all x1, starting transfers between devices, body(): lax.all_to_all(jnp.broadcast_to(sums.reshape(1, 1, 256), (8, 1, 256)), 'z...  9.35 us
    all_to_all x1, starting transfers between devices, body(): p_all = lax.all_to_all(p_sum, ('yh', 'x', 'yl'), 0, 0)  6.67 us
    all_to_all x1, waiting for transfers between devices, body(): lax.all_to_all(jnp.broadcast_to(sums.reshape(1, 1, 256), (8, 1, 256)), 'z...  5.63 us
    transpose x2, other arithmetic, body(): return (residual_next.T, adjoint.T, jnp.sum(sums[0, 128:256]).reshape(1))  2.87 us
  transfers between devices with their start and end apart: 27, of which 10 were waited for; matrix products, arithmetic and copies ran while one was open for 5% of the time, Pallas kernels for 0%

commit v1 on v0

--- a/solution.py
+++ b/solution.py
@@ -42,9 +42,19 @@
     return total
 
 
-def kernel_tiles(w_ref, pos_ref, *refs):
-    z, rows = refs[0:9], refs[9:17]
-    pm_ref, pq_ref, gm_ref, gq_ref, grad_ref, xr, ct, acc = refs[17:]
+def kernel_a(*refs):
+    z, rows = refs[0:5], refs[5:13]
+    p_ref, g_ref, xr, ct = refs[13:]
+    load_rows(xr, ct, rows)
+    for j, ref in enumerate(z):
+        column = (ref[0:256, :], ref[256:512, :])
+        g_ref[j] = add_column(xr, ct, column, p_ref if j else None, p_ref)
+
+
+def kernel_b(w_ref, pos_ref, *refs):
+    f3, b3, f4, b4 = refs[0:4]
+    rows, p_in, ga = refs[4:12], refs[12], refs[13]
+    pm_ref, pq_ref, gm_ref, gq_ref, grad_ref, xr, ct, acc = refs[14:]
     w = w_ref[0]
     z_at, yh_at, x_at, yl_at = (pos_ref[i] for i in range(4))
     load_rows(xr, ct, rows)
@@ -55,10 +65,12 @@
         theirs[2 * slot + yl_at] = block[128:192, :]
         theirs[2 * slot + 1 - yl_at] = block[192:256, :]
 
-    columns = [(ref[0:256, :], ref[256:512, :]) for ref in z[0:7]]
-    columns.append((z[7][...], z[8][...]))
-    for j, column in enumerate(columns):
-        block = add_column(xr, ct, column, acc if j else None, acc)
+    columns = [(ref[0:256, :], ref[256:512, :]) for ref in (f3, b3)] + [(f4[...], b4[...])]
+    for j in range(8):
+        if j < 5:
+            block = ga[j]
+        else:
+            block = add_column(xr, ct, columns[j - 5], p_in if j == 5 else acc, acc)
         emit(gm_ref, gq_ref, lax.rem(z_at + ZD[j], 8), block * w)
     grad = jnp.zeros((256, 256), F32)
     for i, (dy, dx) in enumerate(PD):
@@ -70,7 +82,7 @@
 
 
 def kernel_fold(pos_ref, mine, theirs, base, grad, *refs):
-    rows, out = refs[0:8], refs[21]
+    rows, out = refs[0:8], refs[32]
     yh_at, x_at, yl_at = (pos_ref[i] for i in range(1, 4))
     curve = jnp.zeros((128, 256), F32)
     for ref, (dy, dx) in zip(rows, PD):
@@ -135,16 +147,16 @@
     f4, b4 = send(f3[0:256], "z", 1), send(b3[256:512], "z", -1)
     place = jnp.stack([lax.axis_index(a) for a in ("z", "yh", "x", "yl")]).astype(jnp.int32)
     chunks = (16, 64, 256)
+    tiles = (pltpu.VMEM((2048, 256), BF16), pltpu.VMEM((256, 2048), BF16))
+    p_a, g_a = call(
+        kernel_a, "tiles_a", (z0, f1, b1, f2, b2, *rows), ((256, 2048), (5, 256, 256)), tiles
+    )
     p_mine, p_other, g_mine, g_other, grad = call(
-        kernel_tiles,
-        "tiles",
-        (z0, f1, b1, f2, b2, f3, b3, f4, b4, *rows),
+        kernel_b,
+        "tiles_b",
+        (f3, b3, f4, b4, *rows, p_a, g_a),
         (chunks, chunks, chunks, chunks, (8, 128)),
-        (
-            pltpu.VMEM((2048, 256), BF16),
-            pltpu.VMEM((256, 2048), BF16),
-            pltpu.VMEM((256, 2048), F32),
-        ),
+        (*tiles, pltpu.VMEM((256, 2048), F32)),
         (weight, place),
     )
 
@@ -156,7 +168,7 @@
     (p_sum,) = call(
         kernel_fold,
         "fold",
-        (p_mine, send(p_other, "core", 1), base, grad, *rows, z0, f1, b1, f2, b2, f3, b3, f4, b4, f1, b1, f2, b2),
+        (p_mine, send(p_other, "core", 1), base, grad, *rows, z0, f1, b1, f2, b2, f3, b3, f4, b4, f1, b1, f2, b2, f3, b3, f1, b1, f2, b2, f3, b3, z0, f4, b4),
         ((16, 72, 256),),
         (),
         (place,),

time: 109 us -> 108 us (level)
  waiting for transfers between devices: 24.2 us -> 20.4 us
  starting transfers between devices: 59.9 us -> 61.7 us
  Pallas kernels: 11.8 us -> 13.5 us
    ppermute x25, waiting for transfers between devices: 18.5 us -> 13.2 us  [send(): return lax.ppermute(value, axis, [(i, (i + step) % n) for i in range(n)])]
    pallas_call x2 -> x3, Pallas kernels: 11.8 us -> 13.5 us  [call(): pl.pallas_call(kernel, out_shape=tuple((jax.ShapeDtypeStruct(s, F32) for...]
    all_to_all x1, waiting for transfers between devices: 5.63 us -> 7.18 us  [body(): lax.all_to_all(jnp.broadcast_to(sums.reshape(1, 1, 256), (8, 1, 256)), 'z...]
    all_to_all x1, starting transfers between devices: 9.35 us -> 10.6 us  [body(): lax.all_to_all(jnp.broadcast_to(sums.reshape(1, 1, 256), (8, 1, 256)), 'z...]
  transfers between devices with their start and end apart: 27 -> 27, of which waited for: 10 -> 7; matrix products, arithmetic and copies ran while one was open for 5% -> 5% of each run, Pallas kernels for 0% -> 5%
where the time goes in v1:
time: 108 us; the launch traced here: 107 us
  starting transfers between devices  61.7 us (57%)
  waiting for transfers between devices  20.4 us (19%)
  Pallas kernels  13.5 us (12%)
  other arithmetic  5.27 us (5%)
  local copies, waits for them, and re-layouts  4.13 us (4%)
  between operations  2.37 us (2%)
    ppermute x25, starting transfers between devices, send(): return lax.ppermute(value, axis, [(i, (i + step) % n) for i in range(n)])  44 us
    pallas_call x3, Pallas kernels, call(): pl.pallas_call(kernel, out_shape=tuple((jax.ShapeDtypeStruct(s, F32) for...  13.5 us
    ppermute x25, waiting for transfers between devices, send(): return lax.ppermute(value, axis, [(i, (i + step) % n) for i in range(n)])  13.2 us
    all_to_all x1, starting transfers between devices, body(): lax.all_to_all(jnp.broadcast_to(sums.reshape(1, 1, 256), (8, 1, 256)), 'z...  10.6 us
    all_to_all x1, waiting for transfers between devices, body(): lax.all_to_all(jnp.broadcast_to(sums.reshape(1, 1, 256), (8, 1, 256)), 'z...  7.18 us
    all_to_all x1, starting transfers between devices, body(): p_all = lax.all_to_all(p_sum, ('yh', 'x', 'yl'), 0, 0)  7 us
    transpose x2, other arithmetic, body(): return (residual_next.T, adjoint.T, jnp.sum(sums[0, 128:256]).reshape(1))  2.87 us
  transfers between devices with their start and end apart: 27, of which 7 were waited for; matrix products, arithmetic and copies ran while one was open for 5% of the time, Pallas kernels for 5%

profile of v1, /device:TPU:2, one launch (start us, length us, event | category | flops | bytes accessed | tf_op | source)
XLA Modules:
  0.0 107.3 jit_solution(14558190539323906233)
XLA Ops:
  0.7 1.3 %constant_dynamic-slice_fusion.11 = (bf16[256,64]{1,0:T(8,128)(2,1)S(1)}, bf16[256,64]{1,0:T(8,128)(2,1)S(1)}, bf16[256,64]{1,0:T(8,128)(2,1)S(1)}, bf16[256,64]...) fusion(bf16[256,256]{1,0:T(8,128)(2,1)} %param.8, ...), kind=kLoop, calls=%fused_computation.47 | loop fusion | bytes 524304 | tf_op jit(solution)/shard_map/dynamic_slice | solution.py:123
  2.9 3.3 %collective-permute-start.2 = (bf16[640,256]{1,0:T(8,128)(2,1)S(1)}, bf16[640,256]{1,0:T(8,128)(2,1)S(1)}, u32[]{:S(2)}, u32[]{:S(2)}) collective-permute-start(bf16[640,256]{1,0:T(8,128)(2,1)S(1)} %pad_maximum_fusion.refs_5_.refs_4_.refs_0_), channel_id=1, source_target_pairs={{0,16},{16,0},{1,17},{17,1},{2,18},{18,2},{3,19},{19,3},{4,20},{20... | collective-permute-start | bytes 983048 | tf_op jit(solution)/shard_map/ppermute | solution.py:22
  6.2 1.5 %collective-permute-start.3 = (bf16[640,256]{1,0:T(8,128)(2,1)S(1)}, bf16[640,256]{1,0:T(8,128)(2,1)S(1)}, u32[]{:S(2)}, u32[]{:S(2)}) collective-permute-start(bf16[640,256]{1,0:T(8,128)(2,1)S(1)} %pad_maximum_fusion.refs_5_.refs_4_.refs_0_), channel_id=1, source_target_pairs={{0,4},{4,8},{8,12},{12,0},{1,5},{5,9},{9,13},{13,1},{2,6},{6,10},{... | collective-permute-start | bytes 983048 | tf_op jit(solution)/shard_map/ppermute | solution.py:22
  8.2 2.0 %collective-permute-start = (bf16[512,256]{1,0:T(8,128)(2,1)S(1)}, bf16[512,256]{1,0:T(8,128)(2,1)S(1)}, u32[]{:S(2)}, u32[]{:S(2)}) collective-permute-start(bf16[512,256]{1,0:T(8,128)(2,1)S(1)} %pad_maximum_fusion.1.refs_0_.refs_8_.refs_29_), channel_id=1, source_target_pairs={{0,32},{32,64},{64,96},{96,128},{128,160},{160,192},{192,224},{224... | collective-permute-start | bytes 786440 | tf_op jit(solution)/shard_map/ppermute | solution.py:22
  10.2 4.0 %collective-permute-start.1 = (bf16[512,256]{1,0:T(8,128)(2,1)S(1)}, bf16[512,256]{1,0:T(8,128)(2,1)S(1)}, u32[]{:S(2)}, u32[]{:S(2)}) collective-permute-start(bf16[512,256]{1,0:T(8,128)(2,1)S(1)} %pad_maximum_fusion.1.refs_0_.refs_8_.refs_29_), channel_id=1, source_target_pairs={{0,224},{32,0},{64,32},{96,64},{128,96},{160,128},{192,160},{224,1... | collective-permute-start | bytes 786440 | tf_op jit(solution)/shard_map/ppermute | solution.py:22
  14.2 5.4 %collective-permute-done.refs_1_.refs_9_.refs_17_.refs_23_ = bf16[512,256]{1,0:T(8,128)(2,1)S(1)} collective-permute-done((bf16[512,256]{1,0:T(8,128)(2,1)S(1)}, bf16[512,256]{1,0:T(8,128)(2,1)S(1)}, u32[]{:S(2)}, u32[]{:S(2)}) %collective-permute-start) | collective-permute-done | bytes 262176 | tf_op jit(solution)/shard_map/ppermute | solution.py:22
  19.6 1.6 %collective-permute-start.7 = (bf16[640,256]{1,0:T(8,128)(2,1)S(1)}, bf16[640,256]{1,0:T(8,128)(2,1)S(1)}, u32[]{:S(2)}, u32[]{:S(2)}) collective-permute-start(bf16[640,256]{1,0:T(8,128)(2,1)S(1)} %collective-permute-done.2.refs_6_.refs_5_.refs_1_), channel_id=1, source_target_pairs={{0,4},{4,8},{8,12},{12,0},{1,5},{5,9},{9,13},{13,1},{2,6},{6,10},{... | collective-permute-start | bytes 983048 | tf_op jit(solution)/shard_map/ppermute | solution.py:22
  21.7 3.2 %collective-permute-start.6 = (bf16[512,256]{1,0:T(8,128)(2,1)S(1)}, bf16[512,256]{1,0:T(8,128)(2,1)S(1)}, u32[]{:S(2)}, u32[]{:S(2)}) collective-permute-start(bf16[512,256]{1,0:T(8,128)(2,1)S(1)} %collective-permute-done.1.refs_2_.refs_10_.refs_18_.refs_24_), channel_id=1, source_target_pairs={{0,224},{32,0},{64,32},{96,64},{128,96},{160,128},{192,160},{224,1... | collective-permute-start | bytes 786440 | tf_op jit(solution)/shard_map/ppermute | solution.py:22
  25.0 4.3 %collective-permute-done.5.refs_3_.refs_11_.refs_19_.refs_25_ = bf16[512,256]{1,0:T(8,128)(2,1)S(1)} collective-permute-done((bf16[512,256]{1,0:T(8,128)(2,1)S(1)}, bf16[512,256]{1,0:T(8,128)(2,1)S(1)}, u32[]{:S(2)}, u32[]{:S(2)}) %collective-permute-start.5) | collective-permute-done | bytes 262176 | tf_op jit(solution)/shard_map/ppermute | solution.py:22
  29.3 2.4 %collective-permute-start.9 = (bf16[512,256]{1,0:T(8,128)(2,1)S(1)}, bf16[512,256]{1,0:T(8,128)(2,1)S(1)}, u32[]{:S(2)}, u32[]{:S(2)}) collective-permute-start(bf16[512,256]{1,0:T(8,128)(2,1)S(1)} %collective-permute-done.5.refs_3_.refs_11_.refs_19_.refs_25_), channel_id=1, source_target_pairs={{0,32},{32,64},{64,96},{96,128},{128,160},{160,192},{192,224},{224... | collective-permute-start | bytes 786440 | tf_op jit(solution)/shard_map/ppermute | solution.py:22
  31.8 0.9 collective-permute-start.10
  32.7 1.5 %collective-permute-start.13 = (bf16[640,256]{1,0:T(8,128)(2,1)S(1)}, bf16[640,256]{1,0:T(8,128)(2,1)}, u32[]{:S(2)}, u32[]{:S(2)}) collective-permute-start(bf16[640,256]{1,0:T(8,128)(2,1)S(1)} %collective-permute-done.3.refs_7_.refs_6_.refs_2_), channel_id=1, source_target_pairs={{0,4},{4,8},{8,12},{12,0},{1,5},{5,9},{9,13},{13,1},{2,6},{6,10},{... | collective-permute-start | bytes 983048 | tf_op jit(solution)/shard_map/ppermute | solution.py:22
  34.1 1.5 %collective-permute-start.14 = (bf16[640,256]{1,0:T(8,128)(2,1)}, bf16[640,256]{1,0:T(8,128)(2,1)}, u32[]{:S(2)}, u32[]{:S(2)}) collective-permute-start(bf16[640,256]{1,0:T(8,128)(2,1)} %collective-permute-done.8.refs_10_.refs_9_.refs_5_), channel_id=1, source_target_pairs={{0,12},{4,0},{8,4},{12,8},{1,13},{5,1},{9,5},{13,9},{2,14},{6,2},{... | collective-permute-start | bytes 983048 | tf_op jit(solution)/shard_map/ppermute | solution.py:22
  35.6 1.4 %collective-permute-done.9.refs_0_.refs_13_.refs_21_.refs_27_ = bf16[512,256]{1,0:T(8,128)(2,1)S(1)} collective-permute-done((bf16[512,256]{1,0:T(8,128)(2,1)S(1)}, bf16[512,256]{1,0:T(8,128)(2,1)S(1)}, u32[]{:S(2)}, u32[]{:S(2)}) %collective-permute-start.9) | collective-permute-done | bytes 262176 | tf_op jit(solution)/shard_map/ppermute | solution.py:22
  37.7 2.2 %collective-permute-start.11 = (bf16[256,256]{1,0:T(8,128)(2,1)}, bf16[256,256]{1,0:T(8,128)(2,1)}, u32[]{:S(2)}, u32[]{:S(2)}) collective-permute-start(bf16[256,256]{1,0:T(8,128)(2,1)} %slice.65), channel_id=1, source_target_pairs={{0,32},{32,64},{64,96},{96,128},{128,160},{160,192},{192,224},{224... | collective-permute-start | bytes 393224 | tf_op jit(solution)/shard_map/ppermute | solution.py:22
  40.6 1.0 collective-permute-start.12
  42.4 5.5 %tiles_a.1 = (f32[256,2048]{1,0:T(8,128)S(1)}, f32[5,256,256]{2,1,0:T(8,128)S(1)}) custom-call(bf16[512,256]{1,0:T(8,128)(2,1)S(1)} %pad_maximum_fusion.1.refs_0_.refs_8_.refs_29_, bf16[512,256]{1,0:T(8,128)(2,1)S(1)} %collective-permute-done.refs_1_.refs_9_.refs_17_.refs_23_, bf16[512,256]{1,0:T(8,128)(2,1)S(1)} %collective-permute-done.1.refs_2_.refs_10_.refs_18_.refs_24_, ...), custom_call_target="tpu_custom_call" | custom-call | tf_op jit(solution)/shard_map/tiles_a/pallas_call | solution.py:104
  47.9 5.2 %tiles_b.1 = (f32[16,64,256]{2,1,0:T(8,128)S(1)}, f32[16,64,256]{2,1,0:T(8,128)S(1)}, f32[16,64,256]{2,1,0:T(8,128)S(1)}, f32[16,64,256]{2,1,0:T(8,128)}, f32[8,128]{1,0:T(8,128)S(1)}) custom-call(f32[1]{0:T(128)S(6)} %mul.101.w_ref, s32[4]{0:T(128)S(1)} %pad_add_fusion.pos_ref, ...), custom_call_target="tpu_custom_call" | custom-call | tf_op jit(solution)/shard_map/tiles_b/pallas_call | solution.py:104
  53.7 0.9 fusion.1
  54.8 1.0 collective-permute-done.15.theirs
  55.8 2.8 %fold.1 = f32[16,72,256]{2,1,0:T(8,128)} custom-call(s32[4]{0:T(128)S(1)} %pad_add_fusion.pos_ref, f32[16,64,256]{2,1,0:T(8,128)S(1)} %get-tuple-element.41.mine, f32[16,64,256]{2,1,0:T(8,128)S(1)} %collective-permute-done.15.theirs, f32[8,128]{1,0:T(8,128)S(1)} %select_maximum_fusion.base, f32[8,128]{1,0:T(8,128)S(1)} %get-tuple-element.43.grad, ...), custom_call_target="tpu_custom_call" | custom-call | tf_op jit(solution)/shard_map/fold/pallas_call | solution.py:104
  58.7 7.0 %all-to-all-start = ((f32[16,72,256]{2,1,0:T(8,128)}), f32[16,72,256]{2,1,0:T(8,128)S(1)}, u32[]{:S(2)}, u32[]{:S(2)}) async-start(f32[16,72,256]{2,1,0:T(8,128)} %fold.1), calls=%async_computation | async-start | bytes 2359296 | tf_op jit(solution)/shard_map/all_to_all | solution.py:178
  66.0 2.0 %collective-permute-start.18 = (f32[2,64,256]{2,1,0:T(8,128)S(1)}, f32[2,64,256]{2,1,0:T(8,128)S(1)}, u32[]{:S(2)}, u32[]{:S(2)}) collective-permute-start(f32[2,64,256]{2,1,0:T(8,128)S(1)} %reverse_select_fusion.6), channel_id=1, source_target_pairs={{0,224},{32,0},{64,32},{96,64},{128,96},{160,128},{192,160},{224,1... | collective-permute-start | bytes 393224 | tf_op jit(solution)/shard_map/ppermute | solution.py:22
  68.2 4.4 %collective-permute-start.19 = (f32[2,64,256]{2,1,0:T(8,128)S(1)}, f32[2,64,256]{2,1,0:T(8,128)S(1)}, u32[]{:S(2)}, u32[]{:S(2)}) collective-permute-start(f32[2,64,256]{2,1,0:T(8,128)S(1)} %reverse_select_fusion.5), channel_id=1, source_target_pairs={{0,128},{32,160},{64,192},{96,224},{128,0},{160,32},{192,64},{224,... | collective-permute-start | bytes 393224 | tf_op jit(solution)/shard_map/ppermute | solution.py:22
  72.6 2.2 %collective-permute-start.20 = (f32[2,64,256]{2,1,0:T(8,128)S(1)}, f32[2,64,256]{2,1,0:T(8,128)S(1)}, u32[]{:S(2)}, u32[]{:S(2)}) collective-permute-start(f32[2,64,256]{2,1,0:T(8,128)S(1)} %reverse_select_fusion.4), channel_id=1, source_target_pairs={{0,96},{32,128},{64,160},{96,192},{128,224},{160,0},{192,32},{224,... | collective-permute-start | bytes 393224 | tf_op jit(solution)/shard_map/ppermute | solution.py:22
  74.8 3.2 %collective-permute-start.21 = (f32[2,64,256]{2,1,0:T(8,128)S(1)}, f32[2,64,256]{2,1,0:T(8,128)S(1)}, u32[]{:S(2)}, u32[]{:S(2)}) collective-permute-start(f32[2,64,256]{2,1,0:T(8,128)S(1)} %reverse_select_fusion.3), channel_id=1, source_target_pairs={{0,160},{32,192},{64,224},{96,0},{128,32},{160,64},{192,96},{224,1... | collective-permute-start | bytes 393224 | tf_op jit(solution)/shard_map/ppermute | solution.py:22
  78.6 3.7 %collective-permute-start.23 = (f32[2,64,256]{2,1,0:T(8,128)S(1)}, f32[2,64,256]{2,1,0:T(8,128)S(1)}, u32[]{:S(2)}, u32[]{:S(2)}) collective-permute-start(f32[2,64,256]{2,1,0:T(8,128)S(1)} %reverse_select_fusion.1), channel_id=1, source_target_pairs={{0,192},{32,224},{64,0},{96,32},{128,64},{160,96},{192,128},{224,1... | collective-permute-start | bytes 393224 | tf_op jit(solution)/shard_map/ppermute | solution.py:22
  83.1 10.6 %all-to-all-start.1 = ((f32[8,1,256]{2,1,0:T(1,128)}), f32[8,1,256]{2,1,0:T(1,128)S(1)}, u32[]{:S(2)}, u32[]{:S(2)}) async-start(f32[8,1,256]{2,1,0:T(1,128)} %broadcast_in_dim.2), calls=%async_computation.1 | async-start | bytes 16384 | tf_op jit(solution)/shard_map/all_to_all | solution.py:195
  94.3 7.2 %all-to-all-done.1 = f32[8,1,256]{2,1,0:T(1,128)S(1)} async-done(((f32[8,1,256]{2,1,0:T(1,128)}), f32[8,1,256]{2,1,0:T(1,128)S(1)}, u32[]{:S(2)}, u32[]{:S(2)}) %all-to-all-start.1) | async-done | bytes 8224 | tf_op jit(solution)/shard_map/all_to_all | solution.py:195
  101.6 1.5 %collective-permute-start.24 = (f32[64,256]{1,0:T(8,128)S(1)}, f32[64,256]{1,0:T(8,128)S(1)}, u32[]{:S(2)}, u32[]{:S(2)}) collective-permute-start(f32[64,256]{1,0:T(8,128)S(1)} %slice_bitcast_fusion), channel_id=1, source_target_pairs={{0,2},{2,0},{1,3},{3,1},{4,6},{6,4},{5,7},{7,5},{8,10},{10,8},{9,1... | collective-permute-start | bytes 196616 | tf_op jit(solution)/shard_map/ppermute | solution.py:22
  103.2 1.5 %fusion.5 = f32[256,64]{0,1:T(8,128)} fusion(f32[64,256]{1,0:T(8,128)S(1)} %slice_reduce_fusion, f32[256,64]{0,1:T(8,128)S(1)} %copy-done.5, f32[]{:T(128)} %bitcast.45, f32[64]{0:T(128)S(1)} %fusion.11, bf16[256,256]{1,0:T(8,128)(2,1)} %copy-done.2), kind=kLoop, calls=%fused_computation.20 | loop fusion | flops 81920 | bytes 229636 | tf_op jit(solution)/shard_map/transpose | solution.py:203
  105.9 1.4 %fusion.8 = f32[256,64]{0,1:T(8,128)} fusion(f32[64,256]{1,0:T(8,128)S(1)} %collective-permute-done.24, f32[2,64,256]{2,1,0:T(8,128)S(1)} %fusion, bf16[256,256]{1,0:T(8,128)(2,1)} %copy-done.3, f32[]{:T(128)} %bitcast.46), kind=kLoop, calls=%fused_computation.25 | loop fusion | flops 65536 | bytes 229380 | tf_op jit(solution)/shard_map/transpose | solution.py:203
  (84 shorter events, 7.4 us)
Async XLA Ops:
  2.8 5.4 %copy-start.2 = (bf16[256,256]{1,0:T(8,128)(2,1)}, bf16[256,256]{1,0:T(8,128)(2,1)S(1)}, u32[]{:S(2)}) copy-start(bf16[256,256]{1,0:T(8,128)(2,1)S(1)} %maximum_bitcast_fusion) | copy-start | bytes 393220
  2.8 37.0 %copy-start.3 = (bf16[256,256]{1,0:T(8,128)(2,1)}, bf16[256,256]{1,0:T(8,128)(2,1)S(1)}, u32[]{:S(2)}) copy-start(bf16[256,256]{1,0:T(8,128)(2,1)S(1)} %maximum_bitcast_fusion.1) | copy-start | bytes 393220
  2.9 16.7 %collective-permute-start.2 = (bf16[640,256]{1,0:T(8,128)(2,1)S(1)}, bf16[640,256]{1,0:T(8,128)(2,1)S(1)}, u32[]{:S(2)}, u32[]{:S(2)}) collective-permute-start(bf16[640,256]{1,0:T(8,128)(2,1)S(1)} %pad_maximum_fusion.refs_5_.refs_4_.refs_0_), channel_id=1, source_target_pairs={{0,16},{16,0},{1,17},{17,1},{2,18},{18,2},{3,19},{19,3},{4,20},{20... | collective-permute-start | bytes 983048 | tf_op jit(solution)/shard_map/ppermute | solution.py:22
  6.2 13.5 %collective-permute-start.3 = (bf16[640,256]{1,0:T(8,128)(2,1)S(1)}, bf16[640,256]{1,0:T(8,128)(2,1)S(1)}, u32[]{:S(2)}, u32[]{:S(2)}) collective-permute-start(bf16[640,256]{1,0:T(8,128)(2,1)S(1)} %pad_maximum_fusion.refs_5_.refs_4_.refs_0_), channel_id=1, source_target_pairs={{0,4},{4,8},{8,12},{12,0},{1,5},{5,9},{9,13},{13,1},{2,6},{6,10},{... | collective-permute-start | bytes 983048 | tf_op jit(solution)/shard_map/ppermute | solution.py:22
  7.7 12.0 %collective-permute-start.4 = (bf16[640,256]{1,0:T(8,128)(2,1)S(1)}, bf16[640,256]{1,0:T(8,128)(2,1)S(1)}, u32[]{:S(2)}, u32[]{:S(2)}) collective-permute-start(bf16[640,256]{1,0:T(8,128)(2,1)S(1)} %pad_maximum_fusion.refs_5_.refs_4_.refs_0_), channel_id=1, source_target_pairs={{0,12},{4,0},{8,4},{12,8},{1,13},{5,1},{9,5},{13,9},{2,14},{6,2},{... | collective-permute-start | bytes 983048 | tf_op jit(solution)/shard_map/ppermute | solution.py:22
  8.2 11.4 %collective-permute-start = (bf16[512,256]{1,0:T(8,128)(2,1)S(1)}, bf16[512,256]{1,0:T(8,128)(2,1)S(1)}, u32[]{:S(2)}, u32[]{:S(2)}) collective-permute-start(bf16[512,256]{1,0:T(8,128)(2,1)S(1)} %pad_maximum_fusion.1.refs_0_.refs_8_.refs_29_), channel_id=1, source_target_pairs={{0,32},{32,64},{64,96},{96,128},{128,160},{160,192},{192,224},{224... | collective-permute-start | bytes 786440 | tf_op jit(solution)/shard_map/ppermute | solution.py:22
  10.2 9.4 %collective-permute-start.1 = (bf16[512,256]{1,0:T(8,128)(2,1)S(1)}, bf16[512,256]{1,0:T(8,128)(2,1)S(1)}, u32[]{:S(2)}, u32[]{:S(2)}) collective-permute-start(bf16[512,256]{1,0:T(8,128)(2,1)S(1)} %pad_maximum_fusion.1.refs_0_.refs_8_.refs_29_), channel_id=1, source_target_pairs={{0,224},{32,0},{64,32},{96,64},{128,96},{160,128},{192,160},{224,1... | collective-permute-start | bytes 786440 | tf_op jit(solution)/shard_map/ppermute | solution.py:22
  19.6 9.7 %collective-permute-start.7 = (bf16[640,256]{1,0:T(8,128)(2,1)S(1)}, bf16[640,256]{1,0:T(8,128)(2,1)S(1)}, u32[]{:S(2)}, u32[]{:S(2)}) collective-permute-start(bf16[640,256]{1,0:T(8,128)(2,1)S(1)} %collective-permute-done.2.refs_6_.refs_5_.refs_1_), channel_id=1, source_target_pairs={{0,4},{4,8},{8,12},{12,0},{1,5},{5,9},{9,13},{13,1},{2,6},{6,10},{... | collective-permute-start | bytes 983048 | tf_op jit(solution)/shard_map/ppermute | solution.py:22
  21.2 8.1 %collective-permute-start.8 = (bf16[640,256]{1,0:T(8,128)(2,1)S(1)}, bf16[640,256]{1,0:T(8,128)(2,1)}, u32[]{:S(2)}, u32[]{:S(2)}) collective-permute-start(bf16[640,256]{1,0:T(8,128)(2,1)S(1)} %collective-permute-done.2.refs_6_.refs_5_.refs_1_), channel_id=1, source_target_pairs={{0,12},{4,0},{8,4},{12,8},{1,13},{5,1},{9,5},{13,9},{2,14},{6,2},{... | collective-permute-start | bytes 983048 | tf_op jit(solution)/shard_map/ppermute | solution.py:22
  21.7 7.6 %collective-permute-start.5 = (bf16[512,256]{1,0:T(8,128)(2,1)S(1)}, bf16[512,256]{1,0:T(8,128)(2,1)S(1)}, u32[]{:S(2)}, u32[]{:S(2)}) collective-permute-start(bf16[512,256]{1,0:T(8,128)(2,1)S(1)} %collective-permute-done.refs_1_.refs_9_.refs_17_.refs_23_), channel_id=1, source_target_pairs={{0,32},{32,64},{64,96},{96,128},{128,160},{160,192},{192,224},{224... | collective-permute-start | bytes 786440 | tf_op jit(solution)/shard_map/ppermute | solution.py:22
  21.7 7.6 %collective-permute-start.6 = (bf16[512,256]{1,0:T(8,128)(2,1)S(1)}, bf16[512,256]{1,0:T(8,128)(2,1)S(1)}, u32[]{:S(2)}, u32[]{:S(2)}) collective-permute-start(bf16[512,256]{1,0:T(8,128)(2,1)S(1)} %collective-permute-done.1.refs_2_.refs_10_.refs_18_.refs_24_), channel_id=1, source_target_pairs={{0,224},{32,0},{64,32},{96,64},{128,96},{160,128},{192,160},{224,1... | collective-permute-start | bytes 786440 | tf_op jit(solution)/shard_map/ppermute | solution.py:22
  29.3 7.7 %collective-permute-start.9 = (bf16[512,256]{1,0:T(8,128)(2,1)S(1)}, bf16[512,256]{1,0:T(8,128)(2,1)S(1)}, u32[]{:S(2)}, u32[]{:S(2)}) collective-permute-start(bf16[512,256]{1,0:T(8,128)(2,1)S(1)} %collective-permute-done.5.refs_3_.refs_11_.refs_19_.refs_25_), channel_id=1, source_target_pairs={{0,32},{32,64},{64,96},{96,128},{128,160},{160,192},{192,224},{224... | collective-permute-start | bytes 786440 | tf_op jit(solution)/shard_map/ppermute | solution.py:22
  31.8 8.1 %collective-permute-start.10 = (bf16[512,256]{1,0:T(8,128)(2,1)S(1)}, bf16[512,256]{1,0:T(8,128)(2,1)S(1)}, u32[]{:S(2)}, u32[]{:S(2)}) collective-permute-start(bf16[512,256]{1,0:T(8,128)(2,1)S(1)} %collective-permute-done.6.refs_4_.refs_12_.refs_20_.refs_26_), channel_id=1, source_target_pairs={{0,224},{32,0},{64,32},{96,64},{128,96},{160,128},{192,160},{224,1... | collective-permute-start | bytes 786440 | tf_op jit(solution)/shard_map/ppermute | solution.py:22
  32.7 9.7 %collective-permute-start.13 = (bf16[640,256]{1,0:T(8,128)(2,1)S(1)}, bf16[640,256]{1,0:T(8,128)(2,1)}, u32[]{:S(2)}, u32[]{:S(2)}) collective-permute-start(bf16[640,256]{1,0:T(8,128)(2,1)S(1)} %collective-permute-done.3.refs_7_.refs_6_.refs_2_), channel_id=1, source_target_pairs={{0,4},{4,8},{8,12},{12,0},{1,5},{5,9},{9,13},{13,1},{2,6},{6,10},{... | collective-permute-start | bytes 983048 | tf_op jit(solution)/shard_map/ppermute | solution.py:22
  34.1 8.2 %collective-permute-start.14 = (bf16[640,256]{1,0:T(8,128)(2,1)}, bf16[640,256]{1,0:T(8,128)(2,1)}, u32[]{:S(2)}, u32[]{:S(2)}) collective-permute-start(bf16[640,256]{1,0:T(8,128)(2,1)} %collective-permute-done.8.refs_10_.refs_9_.refs_5_), channel_id=1, source_target_pairs={{0,12},{4,0},{8,4},{12,8},{1,13},{5,1},{9,5},{13,9},{2,14},{6,2},{... | collective-permute-start | bytes 983048 | tf_op jit(solution)/shard_map/ppermute | solution.py:22
  37.7 10.2 %collective-permute-start.11 = (bf16[256,256]{1,0:T(8,128)(2,1)}, bf16[256,256]{1,0:T(8,128)(2,1)}, u32[]{:S(2)}, u32[]{:S(2)}) collective-permute-start(bf16[256,256]{1,0:T(8,128)(2,1)} %slice.65), channel_id=1, source_target_pairs={{0,32},{32,64},{64,96},{96,128},{128,160},{160,192},{192,224},{224... | collective-permute-start | bytes 393224 | tf_op jit(solution)/shard_map/ppermute | solution.py:22
  40.6 7.3 %collective-permute-start.12 = (bf16[256,256]{1,0:T(8,128)(2,1)}, bf16[256,256]{1,0:T(8,128)(2,1)}, u32[]{:S(2)}, u32[]{:S(2)}) collective-permute-start(bf16[256,256]{1,0:T(8,128)(2,1)} %slice.66), channel_id=1, source_target_pairs={{0,224},{32,0},{64,32},{96,64},{128,96},{160,128},{192,160},{224,1... | collective-permute-start | bytes 393224 | tf_op jit(solution)/shard_map/ppermute | solution.py:22
  47.9 6.7 %copy-start.5 = (f32[256,64]{0,1:T(8,128)S(1)}, f32[256,64]{0,1:T(8,128)}, u32[]{:S(2)}) copy-start(f32[256,64]{0,1:T(8,128)} %param.9) | copy-start | bytes 196612
  53.1 5.4 %copy-start = (f32[16,64,256]{2,1,0:T(8,128)}, f32[16,64,256]{2,1,0:T(8,128)S(1)}, u32[]{:S(2)}) copy-start(f32[16,64,256]{2,1,0:T(8,128)S(1)} %get-tuple-element.46) | copy-start | bytes 3145732
  53.1 2.7 %collective-permute-start.15 = (f32[16,64,256]{2,1,0:T(8,128)S(1)}, f32[16,64,256]{2,1,0:T(8,128)S(1)}, u32[]{:S(2)}, u32[]{:S(2)}) collective-permute-start(f32[16,64,256]{2,1,0:T(8,128)S(1)} %get-tuple-element.42), channel_id=1, source_target_pairs={{0,1},{1,0},{2,3},{3,2},{4,5},{5,4},{6,7},{7,6},{8,9},{9,8},{10,11... | collective-permute-start | bytes 3145736 | tf_op jit(solution)/shard_map/ppermute | solution.py:22
  58.5 7.1 %collective-permute-start.16 = (f32[16,64,256]{2,1,0:T(8,128)}, f32[16,64,256]{2,1,0:T(8,128)S(1)}, u32[]{:S(2)}, u32[]{:S(2)}) collective-permute-start(f32[16,64,256]{2,1,0:T(8,128)} %get-tuple-element.47), channel_id=1, source_target_pairs={{0,1},{1,0},{2,3},{3,2},{4,5},{5,4},{6,7},{7,6},{8,9},{9,8},{10,11... | collective-permute-start | bytes 3145736 | tf_op jit(solution)/shard_map/ppermute | solution.py:22
  58.7 7.0 %copy-start.1 = (f32[16,64,256]{2,1,0:T(8,128)S(1)}, f32[16,64,256]{2,1,0:T(8,128)}, u32[]{:S(2)}) copy-start(f32[16,64,256]{2,1,0:T(8,128)} %copy-done) | copy-start | bytes 3145732
  58.7 23.6 %all-to-all-start = ((f32[16,72,256]{2,1,0:T(8,128)}), f32[16,72,256]{2,1,0:T(8,128)S(1)}, u32[]{:S(2)}, u32[]{:S(2)}) async-start(f32[16,72,256]{2,1,0:T(8,128)} %fold.1), calls=%async_computation | async-start | bytes 2359296 | tf_op jit(solution)/shard_map/all_to_all | solution.py:178
  66.0 12.1 %collective-permute-start.18 = (f32[2,64,256]{2,1,0:T(8,128)S(1)}, f32[2,64,256]{2,1,0:T(8,128)S(1)}, u32[]{:S(2)}, u32[]{:S(2)}) collective-permute-start(f32[2,64,256]{2,1,0:T(8,128)S(1)} %reverse_select_fusion.6), channel_id=1, source_target_pairs={{0,224},{32,0},{64,32},{96,64},{128,96},{160,128},{192,160},{224,1... | collective-permute-start | bytes 393224 | tf_op jit(solution)/shard_map/ppermute | solution.py:22
  68.0 10.6 %collective-permute-start.17 = (f32[2,64,256]{2,1,0:T(8,128)S(1)}, f32[2,64,256]{2,1,0:T(8,128)S(1)}, u32[]{:S(2)}, u32[]{:S(2)}) collective-permute-start(f32[2,64,256]{2,1,0:T(8,128)S(1)} %reverse_select_fusion.7), channel_id=1, source_target_pairs={{0,32},{32,64},{64,96},{96,128},{128,160},{160,192},{192,224},{224... | collective-permute-start | bytes 393224 | tf_op jit(solution)/shard_map/ppermute | solution.py:22
  68.2 25.6 %collective-permute-start.19 = (f32[2,64,256]{2,1,0:T(8,128)S(1)}, f32[2,64,256]{2,1,0:T(8,128)S(1)}, u32[]{:S(2)}, u32[]{:S(2)}) collective-permute-start(f32[2,64,256]{2,1,0:T(8,128)S(1)} %reverse_select_fusion.5), channel_id=1, source_target_pairs={{0,128},{32,160},{64,192},{96,224},{128,0},{160,32},{192,64},{224,... | collective-permute-start | bytes 393224 | tf_op jit(solution)/shard_map/ppermute | solution.py:22
  72.6 21.2 %collective-permute-start.20 = (f32[2,64,256]{2,1,0:T(8,128)S(1)}, f32[2,64,256]{2,1,0:T(8,128)S(1)}, u32[]{:S(2)}, u32[]{:S(2)}) collective-permute-start(f32[2,64,256]{2,1,0:T(8,128)S(1)} %reverse_select_fusion.4), channel_id=1, source_target_pairs={{0,96},{32,128},{64,160},{96,192},{128,224},{160,0},{192,32},{224,... | collective-permute-start | bytes 393224 | tf_op jit(solution)/shard_map/ppermute | solution.py:22
  74.8 19.0 %collective-permute-start.21 = (f32[2,64,256]{2,1,0:T(8,128)S(1)}, f32[2,64,256]{2,1,0:T(8,128)S(1)}, u32[]{:S(2)}, u32[]{:S(2)}) collective-permute-start(f32[2,64,256]{2,1,0:T(8,128)S(1)} %reverse_select_fusion.3), channel_id=1, source_target_pairs={{0,160},{32,192},{64,224},{96,0},{128,32},{160,64},{192,96},{224,1... | collective-permute-start | bytes 393224 | tf_op jit(solution)/shard_map/ppermute | solution.py:22
  78.1 15.8 %collective-permute-start.22 = (f32[2,64,256]{2,1,0:T(8,128)S(1)}, f32[2,64,256]{2,1,0:T(8,128)S(1)}, u32[]{:S(2)}, u32[]{:S(2)}) collective-permute-start(f32[2,64,256]{2,1,0:T(8,128)S(1)} %reverse_select_fusion.2), channel_id=1, source_target_pairs={{0,64},{32,96},{64,128},{96,160},{128,192},{160,224},{192,0},{224,... | collective-permute-start | bytes 393224 | tf_op jit(solution)/shard_map/ppermute | solution.py:22
  78.6 15.7 %collective-permute-start.23 = (f32[2,64,256]{2,1,0:T(8,128)S(1)}, f32[2,64,256]{2,1,0:T(8,128)S(1)}, u32[]{:S(2)}, u32[]{:S(2)}) collective-permute-start(f32[2,64,256]{2,1,0:T(8,128)S(1)} %reverse_select_fusion.1), channel_id=1, source_target_pairs={{0,192},{32,224},{64,0},{96,32},{128,64},{160,96},{192,128},{224,1... | collective-permute-start | bytes 393224 | tf_op jit(solution)/shard_map/ppermute | solution.py:22
  83.1 18.4 %all-to-all-start.1 = ((f32[8,1,256]{2,1,0:T(1,128)}), f32[8,1,256]{2,1,0:T(1,128)S(1)}, u32[]{:S(2)}, u32[]{:S(2)}) async-start(f32[8,1,256]{2,1,0:T(1,128)} %broadcast_in_dim.2), calls=%async_computation.1 | async-start | bytes 16384 | tf_op jit(solution)/shard_map/all_to_all | solution.py:195
  101.6 4.4 %collective-permute-start.24 = (f32[64,256]{1,0:T(8,128)S(1)}, f32[64,256]{1,0:T(8,128)S(1)}, u32[]{:S(2)}, u32[]{:S(2)}) collective-permute-start(f32[64,256]{1,0:T(8,128)S(1)} %slice_bitcast_fusion), channel_id=1, source_target_pairs={{0,2},{2,0},{1,3},{3,1},{4,6},{6,4},{5,7},{7,5},{8,10},{10,8},{9,1... | collective-permute-start | bytes 196616 | tf_op jit(solution)/shard_map/ppermute | solution.py:22
  (1 other events, 2.2 us)

commit v2 on v1

--- a/solution.py
+++ b/solution.py
@@ -137,7 +137,7 @@
     f1, b1 = send(z0, "z", 1), send(z0, "z", -1)
     pf, pb = send(p0, "x", 1), send(p0, "x", -1)
     q0 = send(p0, "yh", 1)
-    f1, b1, q0, pf, pb = lax.optimization_barrier((f1, b1, q0, pf, pb))
+    q0, pf, pb = lax.optimization_barrier((q0, pf, pb))
     f2, b2 = send(f1, "z", 1), send(b1, "z", -1)
     qf, qb = send(q0, "x", 1), send(q0, "x", -1)
     f2, b2, qf, qb = lax.optimization_barrier((f2, b2, qf, qb))

time: 108 us -> 107 us (level)
  waiting for transfers between devices: 20.4 us -> 19.1 us
    ppermute x25, waiting for transfers between devices: 13.2 us -> 11.5 us  [send(): return lax.ppermute(value, axis, [(i, (i + step) % n) for i in range(n)])]
  transfers between devices with their start and end apart: 27 -> 27, of which waited for: 7 -> 8; matrix products, arithmetic and copies ran while one was open for 5% -> 5% of each run, Pallas kernels for 5% -> 5%
where the time goes in v2:
time: 107 us; the launch traced here: 106 us
  starting transfers between devices  61.7 us (58%)
  waiting for transfers between devices  19.1 us (18%)
  Pallas kernels  13.5 us (13%)
  other arithmetic  5.27 us (5%)
  local copies, waits for them, and re-layouts  4.13 us (4%)
  between operations  2.38 us (2%)
    ppermute x25, starting transfers between devices, send(): return lax.ppermute(value, axis, [(i, (i + step) % n) for i in range(n)])  44.9 us
    pallas_call x3, Pallas kernels, call(): pl.pallas_call(kernel, out_shape=tuple((jax.ShapeDtypeStruct(s, F32) for...  13.5 us
    ppermute x25, waiting for transfers between devices, send(): return lax.ppermute(value, axis, [(i, (i + step) % n) for i in range(n)])  11.5 us
    all_to_all x1, starting transfers between devices, body(): lax.all_to_all(jnp.broadcast_to(sums.reshape(1, 1, 256), (8, 1, 256)), 'z...  10.9 us
    all_to_all x1, waiting for transfers between devices, body(): lax.all_to_all(jnp.broadcast_to(sums.reshape(1, 1, 256), (8, 1, 256)), 'z...  7.6 us
    all_to_all x1, starting transfers between devices, body(): p_all = lax.all_to_all(p_sum, ('yh', 'x', 'yl'), 0, 0)  6.01 us
    transpose x2, other arithmetic, body(): return (residual_next.T, adjoint.T, jnp.sum(sums[0, 128:256]).reshape(1))  2.87 us
  transfers between devices with their start and end apart: 27, of which 8 were waited for; matrix products, arithmetic and copies ran while one was open for 5% of the time, Pallas kernels for 5%

profile of v2, /device:TPU:2, one launch (start us, length us, event | category | flops | bytes accessed | tf_op | source)
XLA Modules:
  0.0 106.1 jit_solution(12757161100924750803)
XLA Ops:
  0.7 1.3 %constant_dynamic-slice_fusion.11 = (bf16[256,64]{1,0:T(8,128)(2,1)S(1)}, bf16[256,64]{1,0:T(8,128)(2,1)S(1)}, bf16[256,64]{1,0:T(8,128)(2,1)S(1)}, bf16[256,64]...) fusion(bf16[256,256]{1,0:T(8,128)(2,1)} %param.8, ...), kind=kLoop, calls=%fused_computation.47 | loop fusion | bytes 524304 | tf_op jit(solution)/shard_map/dynamic_slice | solution.py:123
  2.9 3.3 %collective-permute-start.4 = (bf16[640,256]{1,0:T(8,128)(2,1)S(1)}, bf16[640,256]{1,0:T(8,128)(2,1)S(1)}, u32[]{:S(2)}, u32[]{:S(2)}) collective-permute-start(bf16[640,256]{1,0:T(8,128)(2,1)S(1)} %pad_maximum_fusion.refs_5_.refs_4_.refs_0_), channel_id=1, source_target_pairs={{0,16},{16,0},{1,17},{17,1},{2,18},{18,2},{3,19},{19,3},{4,20},{20... | collective-permute-start | bytes 983048 | tf_op jit(solution)/shard_map/ppermute | solution.py:22
  6.2 1.5 %collective-permute-start.5 = (bf16[640,256]{1,0:T(8,128)(2,1)S(1)}, bf16[640,256]{1,0:T(8,128)(2,1)S(1)}, u32[]{:S(2)}, u32[]{:S(2)}) collective-permute-start(bf16[640,256]{1,0:T(8,128)(2,1)S(1)} %pad_maximum_fusion.refs_5_.refs_4_.refs_0_), channel_id=1, source_target_pairs={{0,4},{4,8},{8,12},{12,0},{1,5},{5,9},{9,13},{13,1},{2,6},{6,10},{... | collective-permute-start | bytes 983048 | tf_op jit(solution)/shard_map/ppermute | solution.py:22
  8.2 2.0 %collective-permute-start = (bf16[512,256]{1,0:T(8,128)(2,1)S(1)}, bf16[512,256]{1,0:T(8,128)(2,1)S(1)}, u32[]{:S(2)}, u32[]{:S(2)}) collective-permute-start(bf16[512,256]{1,0:T(8,128)(2,1)S(1)} %pad_maximum_fusion.1.refs_0_.refs_8_.refs_29_), channel_id=1, source_target_pairs={{0,32},{32,64},{64,96},{96,128},{128,160},{160,192},{192,224},{224... | collective-permute-start | bytes 786440 | tf_op jit(solution)/shard_map/ppermute | solution.py:22
  10.2 4.0 %collective-permute-start.2 = (bf16[512,256]{1,0:T(8,128)(2,1)S(1)}, bf16[512,256]{1,0:T(8,128)(2,1)S(1)}, u32[]{:S(2)}, u32[]{:S(2)}) collective-permute-start(bf16[512,256]{1,0:T(8,128)(2,1)S(1)} %pad_maximum_fusion.1.refs_0_.refs_8_.refs_29_), channel_id=1, source_target_pairs={{0,224},{32,0},{64,32},{96,64},{128,96},{160,128},{192,160},{224,1... | collective-permute-start | bytes 786440 | tf_op jit(solution)/shard_map/ppermute | solution.py:22
  14.2 1.1 %collective-permute-done.5.refs_7_.refs_6_.refs_2_ = bf16[640,256]{1,0:T(8,128)(2,1)S(1)} collective-permute-done((bf16[640,256]{1,0:T(8,128)(2,1)S(1)}, bf16[640,256]{1,0:T(8,128)(2,1)S(1)}, u32[]{:S(2)}, u32[]{:S(2)}) %collective-permute-start.5) | collective-permute-done | bytes 327712 | tf_op jit(solution)/shard_map/ppermute | solution.py:22
  15.3 1.2 %collective-permute-done.6.refs_9_.refs_8_.refs_4_ = bf16[640,256]{1,0:T(8,128)(2,1)S(1)} collective-permute-done((bf16[640,256]{1,0:T(8,128)(2,1)S(1)}, bf16[640,256]{1,0:T(8,128)(2,1)S(1)}, u32[]{:S(2)}, u32[]{:S(2)}) %collective-permute-start.6) | collective-permute-done | bytes 327712 | tf_op jit(solution)/shard_map/ppermute | solution.py:22
  16.6 1.2 %collective-permute-start.7 = (bf16[640,256]{1,0:T(8,128)(2,1)S(1)}, bf16[640,256]{1,0:T(8,128)(2,1)S(1)}, u32[]{:S(2)}, u32[]{:S(2)}) collective-permute-start(bf16[640,256]{1,0:T(8,128)(2,1)S(1)} %collective-permute-done.4.refs_6_.refs_5_.refs_1_), channel_id=1, source_target_pairs={{0,4},{4,8},{8,12},{12,0},{1,5},{5,9},{9,13},{13,1},{2,6},{6,10},{... | collective-permute-start | bytes 983048 | tf_op jit(solution)/shard_map/ppermute | solution.py:22
  18.6 1.0 collective-permute-done.refs_1_.refs_9_.refs_17_.refs_23_
  19.6 0.9 collective-permute-start.1
  20.5 4.0 %collective-permute-start.3 = (bf16[512,256]{1,0:T(8,128)(2,1)S(1)}, bf16[512,256]{1,0:T(8,128)(2,1)S(1)}, u32[]{:S(2)}, u32[]{:S(2)}) collective-permute-start(bf16[512,256]{1,0:T(8,128)(2,1)S(1)} %collective-permute-done.2.refs_2_.refs_10_.refs_18_.refs_24_), channel_id=1, source_target_pairs={{0,224},{32,0},{64,32},{96,64},{128,96},{160,128},{192,160},{224,1... | collective-permute-start | bytes 786440 | tf_op jit(solution)/shard_map/ppermute | solution.py:22
  24.5 4.3 %collective-permute-done.1.refs_3_.refs_11_.refs_19_.refs_25_ = bf16[512,256]{1,0:T(8,128)(2,1)S(1)} collective-permute-done((bf16[512,256]{1,0:T(8,128)(2,1)S(1)}, bf16[512,256]{1,0:T(8,128)(2,1)S(1)}, u32[]{:S(2)}, u32[]{:S(2)}) %collective-permute-start.1) | collective-permute-done | bytes 262176 | tf_op jit(solution)/shard_map/ppermute | solution.py:22
  28.9 3.3 %collective-permute-start.10 = (bf16[512,256]{1,0:T(8,128)(2,1)S(1)}, bf16[512,256]{1,0:T(8,128)(2,1)S(1)}, u32[]{:S(2)}, u32[]{:S(2)}) collective-permute-start(bf16[512,256]{1,0:T(8,128)(2,1)S(1)} %collective-permute-done.3.refs_4_.refs_12_.refs_20_.refs_26_), channel_id=1, source_target_pairs={{0,224},{32,0},{64,32},{96,64},{128,96},{160,128},{192,160},{224,1... | collective-permute-start | bytes 786440 | tf_op jit(solution)/shard_map/ppermute | solution.py:22
  32.2 1.2 %collective-permute-start.13 = (bf16[640,256]{1,0:T(8,128)(2,1)S(1)}, bf16[640,256]{1,0:T(8,128)(2,1)}, u32[]{:S(2)}, u32[]{:S(2)}) collective-permute-start(bf16[640,256]{1,0:T(8,128)(2,1)S(1)} %collective-permute-done.5.refs_7_.refs_6_.refs_2_), channel_id=1, source_target_pairs={{0,4},{4,8},{8,12},{12,0},{1,5},{5,9},{9,13},{13,1},{2,6},{6,10},{... | collective-permute-start | bytes 983048 | tf_op jit(solution)/shard_map/ppermute | solution.py:22
  34.2 2.2 %collective-permute-done.9.refs_0_.refs_13_.refs_21_.refs_27_ = bf16[512,256]{1,0:T(8,128)(2,1)S(1)} collective-permute-done((bf16[512,256]{1,0:T(8,128)(2,1)S(1)}, bf16[512,256]{1,0:T(8,128)(2,1)S(1)}, u32[]{:S(2)}, u32[]{:S(2)}) %collective-permute-start.9) | collective-permute-done | bytes 262176 | tf_op jit(solution)/shard_map/ppermute | solution.py:22
  37.8 3.2 %collective-permute-start.12 = (bf16[256,256]{1,0:T(8,128)(2,1)}, bf16[256,256]{1,0:T(8,128)(2,1)}, u32[]{:S(2)}, u32[]{:S(2)}) collective-permute-start(bf16[256,256]{1,0:T(8,128)(2,1)} %slice.66), channel_id=1, source_target_pairs={{0,224},{32,0},{64,32},{96,64},{128,96},{160,128},{192,160},{224,1... | collective-permute-start | bytes 393224 | tf_op jit(solution)/shard_map/ppermute | solution.py:22
  41.8 5.5 %tiles_a.1 = (f32[256,2048]{1,0:T(8,128)S(1)}, f32[5,256,256]{2,1,0:T(8,128)S(1)}) custom-call(bf16[512,256]{1,0:T(8,128)(2,1)S(1)} %pad_maximum_fusion.1.refs_0_.refs_8_.refs_29_, bf16[512,256]{1,0:T(8,128)(2,1)S(1)} %collective-permute-done.refs_1_.refs_9_.refs_17_.refs_23_, bf16[512,256]{1,0:T(8,128)(2,1)S(1)} %collective-permute-done.2.refs_2_.refs_10_.refs_18_.refs_24_, ...), custom_call_target="tpu_custom_call" | custom-call | tf_op jit(solution)/shard_map/tiles_a/pallas_call | solution.py:104
  47.4 5.2 %tiles_b.1 = (f32[16,64,256]{2,1,0:T(8,128)S(1)}, f32[16,64,256]{2,1,0:T(8,128)S(1)}, f32[16,64,256]{2,1,0:T(8,128)S(1)}, f32[16,64,256]{2,1,0:T(8,128)}, f32[8,128]{1,0:T(8,128)S(1)}) custom-call(f32[1]{0:T(128)S(6)} %mul.101.w_ref, s32[4]{0:T(128)S(1)} %pad_add_fusion.pos_ref, ...), custom_call_target="tpu_custom_call" | custom-call | tf_op jit(solution)/shard_map/tiles_b/pallas_call | solution.py:104
  53.2 0.9 fusion.1
  54.2 1.0 collective-permute-done.15.theirs
  55.2 2.8 %fold.1 = f32[16,72,256]{2,1,0:T(8,128)} custom-call(s32[4]{0:T(128)S(1)} %pad_add_fusion.pos_ref, f32[16,64,256]{2,1,0:T(8,128)S(1)} %get-tuple-element.37.mine, f32[16,64,256]{2,1,0:T(8,128)S(1)} %collective-permute-done.15.theirs, f32[8,128]{1,0:T(8,128)S(1)} %select_maximum_fusion.base, f32[8,128]{1,0:T(8,128)S(1)} %get-tuple-element.39.grad, ...), custom_call_target="tpu_custom_call" | custom-call | tf_op jit(solution)/shard_map/fold/pallas_call | solution.py:104
  58.1 6.0 %all-to-all-start = ((f32[16,72,256]{2,1,0:T(8,128)}), f32[16,72,256]{2,1,0:T(8,128)S(1)}, u32[]{:S(2)}, u32[]{:S(2)}) async-start(f32[16,72,256]{2,1,0:T(8,128)} %fold.1), calls=%async_computation | async-start | bytes 2359296 | tf_op jit(solution)/shard_map/all_to_all | solution.py:178
  64.4 1.9 %collective-permute-start.18 = (f32[2,64,256]{2,1,0:T(8,128)S(1)}, f32[2,64,256]{2,1,0:T(8,128)S(1)}, u32[]{:S(2)}, u32[]{:S(2)}) collective-permute-start(f32[2,64,256]{2,1,0:T(8,128)S(1)} %reverse_select_fusion.6), channel_id=1, source_target_pairs={{0,224},{32,0},{64,32},{96,64},{128,96},{160,128},{192,160},{224,1... | collective-permute-start | bytes 393224 | tf_op jit(solution)/shard_map/ppermute | solution.py:22
  66.7 4.5 %collective-permute-start.19 = (f32[2,64,256]{2,1,0:T(8,128)S(1)}, f32[2,64,256]{2,1,0:T(8,128)S(1)}, u32[]{:S(2)}, u32[]{:S(2)}) collective-permute-start(f32[2,64,256]{2,1,0:T(8,128)S(1)} %reverse_select_fusion.5), channel_id=1, source_target_pairs={{0,128},{32,160},{64,192},{96,224},{128,0},{160,32},{192,64},{224,... | collective-permute-start | bytes 393224 | tf_op jit(solution)/shard_map/ppermute | solution.py:22
  71.1 2.0 %collective-permute-start.20 = (f32[2,64,256]{2,1,0:T(8,128)S(1)}, f32[2,64,256]{2,1,0:T(8,128)S(1)}, u32[]{:S(2)}, u32[]{:S(2)}) collective-permute-start(f32[2,64,256]{2,1,0:T(8,128)S(1)} %reverse_select_fusion.4), channel_id=1, source_target_pairs={{0,96},{32,128},{64,160},{96,192},{128,224},{160,0},{192,32},{224,... | collective-permute-start | bytes 393224 | tf_op jit(solution)/shard_map/ppermute | solution.py:22
  73.2 3.4 %collective-permute-start.21 = (f32[2,64,256]{2,1,0:T(8,128)S(1)}, f32[2,64,256]{2,1,0:T(8,128)S(1)}, u32[]{:S(2)}, u32[]{:S(2)}) collective-permute-start(f32[2,64,256]{2,1,0:T(8,128)S(1)} %reverse_select_fusion.3), channel_id=1, source_target_pairs={{0,160},{32,192},{64,224},{96,0},{128,32},{160,64},{192,96},{224,1... | collective-permute-start | bytes 393224 | tf_op jit(solution)/shard_map/ppermute | solution.py:22
  77.2 3.6 %collective-permute-start.23 = (f32[2,64,256]{2,1,0:T(8,128)S(1)}, f32[2,64,256]{2,1,0:T(8,128)S(1)}, u32[]{:S(2)}, u32[]{:S(2)}) collective-permute-start(f32[2,64,256]{2,1,0:T(8,128)S(1)} %reverse_select_fusion.1), channel_id=1, source_target_pairs={{0,192},{32,224},{64,0},{96,32},{128,64},{160,96},{192,128},{224,1... | collective-permute-start | bytes 393224 | tf_op jit(solution)/shard_map/ppermute | solution.py:22
  81.7 10.9 %all-to-all-start.1 = ((f32[8,1,256]{2,1,0:T(1,128)}), f32[8,1,256]{2,1,0:T(1,128)S(1)}, u32[]{:S(2)}, u32[]{:S(2)}) async-start(f32[8,1,256]{2,1,0:T(1,128)} %broadcast_in_dim.2), calls=%async_computation.1 | async-start | bytes 16384 | tf_op jit(solution)/shard_map/all_to_all | solution.py:195
  92.7 7.6 %all-to-all-done.1 = f32[8,1,256]{2,1,0:T(1,128)S(1)} async-done(((f32[8,1,256]{2,1,0:T(1,128)}), f32[8,1,256]{2,1,0:T(1,128)S(1)}, u32[]{:S(2)}, u32[]{:S(2)}) %all-to-all-start.1) | async-done | bytes 8224 | tf_op jit(solution)/shard_map/all_to_all | solution.py:195
  100.3 1.6 %collective-permute-start.24 = (f32[64,256]{1,0:T(8,128)S(1)}, f32[64,256]{1,0:T(8,128)S(1)}, u32[]{:S(2)}, u32[]{:S(2)}) collective-permute-start(f32[64,256]{1,0:T(8,128)S(1)} %slice_bitcast_fusion), channel_id=1, source_target_pairs={{0,2},{2,0},{1,3},{3,1},{4,6},{6,4},{5,7},{7,5},{8,10},{10,8},{9,1... | collective-permute-start | bytes 196616 | tf_op jit(solution)/shard_map/ppermute | solution.py:22
  102.0 1.5 %fusion.5 = f32[256,64]{0,1:T(8,128)} fusion(f32[64,256]{1,0:T(8,128)S(1)} %slice_reduce_fusion, f32[256,64]{0,1:T(8,128)S(1)} %copy-done.5, f32[]{:T(128)} %bitcast.45, f32[64]{0:T(128)S(1)} %fusion.11, bf16[256,256]{1,0:T(8,128)(2,1)} %copy-done.2), kind=kLoop, calls=%fused_computation.20 | loop fusion | flops 81920 | bytes 229636 | tf_op jit(solution)/shard_map/transpose | solution.py:203
  104.7 1.4 %fusion.8 = f32[256,64]{0,1:T(8,128)} fusion(f32[64,256]{1,0:T(8,128)S(1)} %collective-permute-done.24, f32[2,64,256]{2,1,0:T(8,128)S(1)} %fusion, bf16[256,256]{1,0:T(8,128)(2,1)} %copy-done.3, f32[]{:T(128)} %bitcast.46), kind=kLoop, calls=%fused_computation.25 | loop fusion | flops 65536 | bytes 229380 | tf_op jit(solution)/shard_map/transpose | solution.py:203
  (84 shorter events, 8.3 us)
Async XLA Ops:
  2.8 5.4 %copy-start.2 = (bf16[256,256]{1,0:T(8,128)(2,1)}, bf16[256,256]{1,0:T(8,128)(2,1)S(1)}, u32[]{:S(2)}) copy-start(bf16[256,256]{1,0:T(8,128)(2,1)S(1)} %maximum_bitcast_fusion) | copy-start | bytes 393220
  2.8 34.3 %copy-start.3 = (bf16[256,256]{1,0:T(8,128)(2,1)}, bf16[256,256]{1,0:T(8,128)(2,1)S(1)}, u32[]{:S(2)}) copy-start(bf16[256,256]{1,0:T(8,128)(2,1)S(1)} %maximum_bitcast_fusion.1) | copy-start | bytes 393220
  2.9 11.4 %collective-permute-start.4 = (bf16[640,256]{1,0:T(8,128)(2,1)S(1)}, bf16[640,256]{1,0:T(8,128)(2,1)S(1)}, u32[]{:S(2)}, u32[]{:S(2)}) collective-permute-start(bf16[640,256]{1,0:T(8,128)(2,1)S(1)} %pad_maximum_fusion.refs_5_.refs_4_.refs_0_), channel_id=1, source_target_pairs={{0,16},{16,0},{1,17},{17,1},{2,18},{18,2},{3,19},{19,3},{4,20},{20... | collective-permute-start | bytes 983048 | tf_op jit(solution)/shard_map/ppermute | solution.py:22
  6.2 9.2 %collective-permute-start.5 = (bf16[640,256]{1,0:T(8,128)(2,1)S(1)}, bf16[640,256]{1,0:T(8,128)(2,1)S(1)}, u32[]{:S(2)}, u32[]{:S(2)}) collective-permute-start(bf16[640,256]{1,0:T(8,128)(2,1)S(1)} %pad_maximum_fusion.refs_5_.refs_4_.refs_0_), channel_id=1, source_target_pairs={{0,4},{4,8},{8,12},{12,0},{1,5},{5,9},{9,13},{13,1},{2,6},{6,10},{... | collective-permute-start | bytes 983048 | tf_op jit(solution)/shard_map/ppermute | solution.py:22
  7.7 8.9 %collective-permute-start.6 = (bf16[640,256]{1,0:T(8,128)(2,1)S(1)}, bf16[640,256]{1,0:T(8,128)(2,1)S(1)}, u32[]{:S(2)}, u32[]{:S(2)}) collective-permute-start(bf16[640,256]{1,0:T(8,128)(2,1)S(1)} %pad_maximum_fusion.refs_5_.refs_4_.refs_0_), channel_id=1, source_target_pairs={{0,12},{4,0},{8,4},{12,8},{1,13},{5,1},{9,5},{13,9},{2,14},{6,2},{... | collective-permute-start | bytes 983048 | tf_op jit(solution)/shard_map/ppermute | solution.py:22
  8.2 11.4 %collective-permute-start = (bf16[512,256]{1,0:T(8,128)(2,1)S(1)}, bf16[512,256]{1,0:T(8,128)(2,1)S(1)}, u32[]{:S(2)}, u32[]{:S(2)}) collective-permute-start(bf16[512,256]{1,0:T(8,128)(2,1)S(1)} %pad_maximum_fusion.1.refs_0_.refs_8_.refs_29_), channel_id=1, source_target_pairs={{0,32},{32,64},{64,96},{96,128},{128,160},{160,192},{192,224},{224... | collective-permute-start | bytes 786440 | tf_op jit(solution)/shard_map/ppermute | solution.py:22
  10.2 10.3 %collective-permute-start.2 = (bf16[512,256]{1,0:T(8,128)(2,1)S(1)}, bf16[512,256]{1,0:T(8,128)(2,1)S(1)}, u32[]{:S(2)}, u32[]{:S(2)}) collective-permute-start(bf16[512,256]{1,0:T(8,128)(2,1)S(1)} %pad_maximum_fusion.1.refs_0_.refs_8_.refs_29_), channel_id=1, source_target_pairs={{0,224},{32,0},{64,32},{96,64},{128,96},{160,128},{192,160},{224,1... | collective-permute-start | bytes 786440 | tf_op jit(solution)/shard_map/ppermute | solution.py:22
  16.6 12.2 %collective-permute-start.7 = (bf16[640,256]{1,0:T(8,128)(2,1)S(1)}, bf16[640,256]{1,0:T(8,128)(2,1)S(1)}, u32[]{:S(2)}, u32[]{:S(2)}) collective-permute-start(bf16[640,256]{1,0:T(8,128)(2,1)S(1)} %collective-permute-done.4.refs_6_.refs_5_.refs_1_), channel_id=1, source_target_pairs={{0,4},{4,8},{8,12},{12,0},{1,5},{5,9},{9,13},{13,1},{2,6},{6,10},{... | collective-permute-start | bytes 983048 | tf_op jit(solution)/shard_map/ppermute | solution.py:22
  17.7 11.0 %collective-permute-start.8 = (bf16[640,256]{1,0:T(8,128)(2,1)S(1)}, bf16[640,256]{1,0:T(8,128)(2,1)}, u32[]{:S(2)}, u32[]{:S(2)}) collective-permute-start(bf16[640,256]{1,0:T(8,128)(2,1)S(1)} %collective-permute-done.4.refs_6_.refs_5_.refs_1_), channel_id=1, source_target_pairs={{0,12},{4,0},{8,4},{12,8},{1,13},{5,1},{9,5},{13,9},{2,14},{6,2},{... | collective-permute-start | bytes 983048 | tf_op jit(solution)/shard_map/ppermute | solution.py:22
  19.6 9.2 %collective-permute-start.1 = (bf16[512,256]{1,0:T(8,128)(2,1)S(1)}, bf16[512,256]{1,0:T(8,128)(2,1)S(1)}, u32[]{:S(2)}, u32[]{:S(2)}) collective-permute-start(bf16[512,256]{1,0:T(8,128)(2,1)S(1)} %collective-permute-done.refs_1_.refs_9_.refs_17_.refs_23_), channel_id=1, source_target_pairs={{0,32},{32,64},{64,96},{96,128},{128,160},{160,192},{192,224},{224... | collective-permute-start | bytes 786440 | tf_op jit(solution)/shard_map/ppermute | solution.py:22
  20.5 8.3 %collective-permute-start.3 = (bf16[512,256]{1,0:T(8,128)(2,1)S(1)}, bf16[512,256]{1,0:T(8,128)(2,1)S(1)}, u32[]{:S(2)}, u32[]{:S(2)}) collective-permute-start(bf16[512,256]{1,0:T(8,128)(2,1)S(1)} %collective-permute-done.2.refs_2_.refs_10_.refs_18_.refs_24_), channel_id=1, source_target_pairs={{0,224},{32,0},{64,32},{96,64},{128,96},{160,128},{192,160},{224,1... | collective-permute-start | bytes 786440 | tf_op jit(solution)/shard_map/ppermute | solution.py:22
  28.8 7.7 %collective-permute-start.9 = (bf16[512,256]{1,0:T(8,128)(2,1)S(1)}, bf16[512,256]{1,0:T(8,128)(2,1)S(1)}, u32[]{:S(2)}, u32[]{:S(2)}) collective-permute-start(bf16[512,256]{1,0:T(8,128)(2,1)S(1)} %collective-permute-done.1.refs_3_.refs_11_.refs_19_.refs_25_), channel_id=1, source_target_pairs={{0,32},{32,64},{64,96},{96,128},{128,160},{160,192},{192,224},{224... | collective-permute-start | bytes 786440 | tf_op jit(solution)/shard_map/ppermute | solution.py:22
  28.9 8.2 %collective-permute-start.10 = (bf16[512,256]{1,0:T(8,128)(2,1)S(1)}, bf16[512,256]{1,0:T(8,128)(2,1)S(1)}, u32[]{:S(2)}, u32[]{:S(2)}) collective-permute-start(bf16[512,256]{1,0:T(8,128)(2,1)S(1)} %collective-permute-done.3.refs_4_.refs_12_.refs_20_.refs_26_), channel_id=1, source_target_pairs={{0,224},{32,0},{64,32},{96,64},{128,96},{160,128},{192,160},{224,1... | collective-permute-start | bytes 786440 | tf_op jit(solution)/shard_map/ppermute | solution.py:22
  32.2 9.6 %collective-permute-start.13 = (bf16[640,256]{1,0:T(8,128)(2,1)S(1)}, bf16[640,256]{1,0:T(8,128)(2,1)}, u32[]{:S(2)}, u32[]{:S(2)}) collective-permute-start(bf16[640,256]{1,0:T(8,128)(2,1)S(1)} %collective-permute-done.5.refs_7_.refs_6_.refs_2_), channel_id=1, source_target_pairs={{0,4},{4,8},{8,12},{12,0},{1,5},{5,9},{9,13},{13,1},{2,6},{6,10},{... | collective-permute-start | bytes 983048 | tf_op jit(solution)/shard_map/ppermute | solution.py:22
  33.4 8.4 %collective-permute-start.14 = (bf16[640,256]{1,0:T(8,128)(2,1)}, bf16[640,256]{1,0:T(8,128)(2,1)}, u32[]{:S(2)}, u32[]{:S(2)}) collective-permute-start(bf16[640,256]{1,0:T(8,128)(2,1)} %collective-permute-done.8.refs_10_.refs_9_.refs_5_), channel_id=1, source_target_pairs={{0,12},{4,0},{8,4},{12,8},{1,13},{5,1},{9,5},{13,9},{2,14},{6,2},{... | collective-permute-start | bytes 983048 | tf_op jit(solution)/shard_map/ppermute | solution.py:22
  37.1 10.2 %collective-permute-start.11 = (bf16[256,256]{1,0:T(8,128)(2,1)}, bf16[256,256]{1,0:T(8,128)(2,1)}, u32[]{:S(2)}, u32[]{:S(2)}) collective-permute-start(bf16[256,256]{1,0:T(8,128)(2,1)} %slice.65), channel_id=1, source_target_pairs={{0,32},{32,64},{64,96},{96,128},{128,160},{160,192},{192,224},{224... | collective-permute-start | bytes 393224 | tf_op jit(solution)/shard_map/ppermute | solution.py:22
  37.8 9.6 %collective-permute-start.12 = (bf16[256,256]{1,0:T(8,128)(2,1)}, bf16[256,256]{1,0:T(8,128)(2,1)}, u32[]{:S(2)}, u32[]{:S(2)}) collective-permute-start(bf16[256,256]{1,0:T(8,128)(2,1)} %slice.66), channel_id=1, source_target_pairs={{0,224},{32,0},{64,32},{96,64},{128,96},{160,128},{192,160},{224,1... | collective-permute-start | bytes 393224 | tf_op jit(solution)/shard_map/ppermute | solution.py:22
  47.4 6.7 %copy-start.5 = (f32[256,64]{0,1:T(8,128)S(1)}, f32[256,64]{0,1:T(8,128)}, u32[]{:S(2)}) copy-start(f32[256,64]{0,1:T(8,128)} %param.9) | copy-start | bytes 196612
  52.5 5.4 %copy-start = (f32[16,64,256]{2,1,0:T(8,128)}, f32[16,64,256]{2,1,0:T(8,128)S(1)}, u32[]{:S(2)}) copy-start(f32[16,64,256]{2,1,0:T(8,128)S(1)} %get-tuple-element.42) | copy-start | bytes 3145732
  52.5 2.7 %collective-permute-start.15 = (f32[16,64,256]{2,1,0:T(8,128)S(1)}, f32[16,64,256]{2,1,0:T(8,128)S(1)}, u32[]{:S(2)}, u32[]{:S(2)}) collective-permute-start(f32[16,64,256]{2,1,0:T(8,128)S(1)} %get-tuple-element.38), channel_id=1, source_target_pairs={{0,1},{1,0},{2,3},{3,2},{4,5},{5,4},{6,7},{7,6},{8,9},{9,8},{10,11... | collective-permute-start | bytes 3145736 | tf_op jit(solution)/shard_map/ppermute | solution.py:22
  58.0 6.2 %collective-permute-start.16 = (f32[16,64,256]{2,1,0:T(8,128)}, f32[16,64,256]{2,1,0:T(8,128)S(1)}, u32[]{:S(2)}, u32[]{:S(2)}) collective-permute-start(f32[16,64,256]{2,1,0:T(8,128)} %get-tuple-element.43), channel_id=1, source_target_pairs={{0,1},{1,0},{2,3},{3,2},{4,5},{5,4},{6,7},{7,6},{8,9},{9,8},{10,11... | collective-permute-start | bytes 3145736 | tf_op jit(solution)/shard_map/ppermute | solution.py:22
  58.1 6.0 %copy-start.1 = (f32[16,64,256]{2,1,0:T(8,128)S(1)}, f32[16,64,256]{2,1,0:T(8,128)}, u32[]{:S(2)}) copy-start(f32[16,64,256]{2,1,0:T(8,128)} %copy-done) | copy-start | bytes 3145732
  58.1 22.7 %all-to-all-start = ((f32[16,72,256]{2,1,0:T(8,128)}), f32[16,72,256]{2,1,0:T(8,128)S(1)}, u32[]{:S(2)}, u32[]{:S(2)}) async-start(f32[16,72,256]{2,1,0:T(8,128)} %fold.1), calls=%async_computation | async-start | bytes 2359296 | tf_op jit(solution)/shard_map/all_to_all | solution.py:178
  64.4 12.2 %collective-permute-start.18 = (f32[2,64,256]{2,1,0:T(8,128)S(1)}, f32[2,64,256]{2,1,0:T(8,128)S(1)}, u32[]{:S(2)}, u32[]{:S(2)}) collective-permute-start(f32[2,64,256]{2,1,0:T(8,128)S(1)} %reverse_select_fusion.6), channel_id=1, source_target_pairs={{0,224},{32,0},{64,32},{96,64},{128,96},{160,128},{192,160},{224,1... | collective-permute-start | bytes 393224 | tf_op jit(solution)/shard_map/ppermute | solution.py:22
  66.4 10.8 %collective-permute-start.17 = (f32[2,64,256]{2,1,0:T(8,128)S(1)}, f32[2,64,256]{2,1,0:T(8,128)S(1)}, u32[]{:S(2)}, u32[]{:S(2)}) collective-permute-start(f32[2,64,256]{2,1,0:T(8,128)S(1)} %reverse_select_fusion.7), channel_id=1, source_target_pairs={{0,32},{32,64},{64,96},{96,128},{128,160},{160,192},{192,224},{224... | collective-permute-start | bytes 393224 | tf_op jit(solution)/shard_map/ppermute | solution.py:22
  66.7 26.0 %collective-permute-start.19 = (f32[2,64,256]{2,1,0:T(8,128)S(1)}, f32[2,64,256]{2,1,0:T(8,128)S(1)}, u32[]{:S(2)}, u32[]{:S(2)}) collective-permute-start(f32[2,64,256]{2,1,0:T(8,128)S(1)} %reverse_select_fusion.5), channel_id=1, source_target_pairs={{0,128},{32,160},{64,192},{96,224},{128,0},{160,32},{192,64},{224,... | collective-permute-start | bytes 393224 | tf_op jit(solution)/shard_map/ppermute | solution.py:22
  71.1 21.5 %collective-permute-start.20 = (f32[2,64,256]{2,1,0:T(8,128)S(1)}, f32[2,64,256]{2,1,0:T(8,128)S(1)}, u32[]{:S(2)}, u32[]{:S(2)}) collective-permute-start(f32[2,64,256]{2,1,0:T(8,128)S(1)} %reverse_select_fusion.4), channel_id=1, source_target_pairs={{0,96},{32,128},{64,160},{96,192},{128,224},{160,0},{192,32},{224,... | collective-permute-start | bytes 393224 | tf_op jit(solution)/shard_map/ppermute | solution.py:22
  73.2 19.5 %collective-permute-start.21 = (f32[2,64,256]{2,1,0:T(8,128)S(1)}, f32[2,64,256]{2,1,0:T(8,128)S(1)}, u32[]{:S(2)}, u32[]{:S(2)}) collective-permute-start(f32[2,64,256]{2,1,0:T(8,128)S(1)} %reverse_select_fusion.3), channel_id=1, source_target_pairs={{0,160},{32,192},{64,224},{96,0},{128,32},{160,64},{192,96},{224,1... | collective-permute-start | bytes 393224 | tf_op jit(solution)/shard_map/ppermute | solution.py:22
  76.6 16.0 %collective-permute-start.22 = (f32[2,64,256]{2,1,0:T(8,128)S(1)}, f32[2,64,256]{2,1,0:T(8,128)S(1)}, u32[]{:S(2)}, u32[]{:S(2)}) collective-permute-start(f32[2,64,256]{2,1,0:T(8,128)S(1)} %reverse_select_fusion.2), channel_id=1, source_target_pairs={{0,64},{32,96},{64,128},{96,160},{128,192},{160,224},{192,0},{224,... | collective-permute-start | bytes 393224 | tf_op jit(solution)/shard_map/ppermute | solution.py:22
  77.2 15.5 %collective-permute-start.23 = (f32[2,64,256]{2,1,0:T(8,128)S(1)}, f32[2,64,256]{2,1,0:T(8,128)S(1)}, u32[]{:S(2)}, u32[]{:S(2)}) collective-permute-start(f32[2,64,256]{2,1,0:T(8,128)S(1)} %reverse_select_fusion.1), channel_id=1, source_target_pairs={{0,192},{32,224},{64,0},{96,32},{128,64},{160,96},{192,128},{224,1... | collective-permute-start | bytes 393224 | tf_op jit(solution)/shard_map/ppermute | solution.py:22
  81.7 18.6 %all-to-all-start.1 = ((f32[8,1,256]{2,1,0:T(1,128)}), f32[8,1,256]{2,1,0:T(1,128)S(1)}, u32[]{:S(2)}, u32[]{:S(2)}) async-start(f32[8,1,256]{2,1,0:T(1,128)} %broadcast_in_dim.2), calls=%async_computation.1 | async-start | bytes 16384 | tf_op jit(solution)/shard_map/all_to_all | solution.py:195
  100.3 4.4 %collective-permute-start.24 = (f32[64,256]{1,0:T(8,128)S(1)}, f32[64,256]{1,0:T(8,128)S(1)}, u32[]{:S(2)}, u32[]{:S(2)}) collective-permute-start(f32[64,256]{1,0:T(8,128)S(1)} %slice_bitcast_fusion), channel_id=1, source_target_pairs={{0,2},{2,0},{1,3},{3,1},{4,6},{6,4},{5,7},{7,5},{8,10},{10,8},{9,1... | collective-permute-start | bytes 196616 | tf_op jit(solution)/shard_map/ppermute | solution.py:22
  (1 other events, 2.2 us)

commit v3 on v2

--- a/solution.py
+++ b/solution.py
@@ -140,7 +140,7 @@
     q0, pf, pb = lax.optimization_barrier((q0, pf, pb))
     f2, b2 = send(f1, "z", 1), send(b1, "z", -1)
     qf, qb = send(q0, "x", 1), send(q0, "x", -1)
-    f2, b2, qf, qb = lax.optimization_barrier((f2, b2, qf, qb))
+    qf, qb, pf = lax.optimization_barrier((qf, qb, pf))
     f3, b3 = send(f2, "z", 1), send(b2, "z", -1)
     p2, q2 = send(pf, "x", 1), send(qb, "x", -1)
     rows = (p0, q0, pf, qf, pb, qb, p2, q2)

time: 107 us -> 106 us (level)
  starting transfers between devices: 61.7 us -> 57.8 us
  waiting for transfers between devices: 19.1 us -> 22.6 us
    ppermute x25, waiting for transfers between devices: 11.5 us -> 17.1 us  [send(): return lax.ppermute(value, axis, [(i, (i + step) % n) for i in range(n)])]
    all_to_all x1, starting transfers between devices: 10.9 us -> 6.84 us  [body(): lax.all_to_all(jnp.broadcast_to(sums.reshape(1, 1, 256), (8, 1, 256)), 'z...]
    all_to_all x1, waiting for transfers between devices: 7.6 us -> 5.46 us  [body(): lax.all_to_all(jnp.broadcast_to(sums.reshape(1, 1, 256), (8, 1, 256)), 'z...]
    all_to_all x1, starting transfers between devices: 6.01 us -> 7.19 us  [body(): p_all = lax.all_to_all(p_sum, ('yh', 'x', 'yl'), 0, 0)]
    ppermute x25, starting transfers between devices: 44.9 us -> 43.8 us  [send(): return lax.ppermute(value, axis, [(i, (i + step) % n) for i in range(n)])]
  transfers between devices with their start and end apart: 27 -> 27, of which waited for: 8 -> 9; matrix products, arithmetic and copies ran while one was open for 5% -> 5% of each run, Pallas kernels for 5% -> 5%
where the time goes in v3:
time: 106 us
  starting transfers between devices  57.8 us (55%)
  waiting for transfers between devices  22.6 us (21%)
  Pallas kernels  13.5 us (13%)
  other arithmetic  5.27 us (5%)
  local copies, waits for them, and re-layouts  4.13 us (4%)
  between operations  2.35 us (2%)
    ppermute x25, starting transfers between devices, send(): return lax.ppermute(value, axis, [(i, (i + step) % n) for i in range(n)])  43.8 us
    ppermute x25, waiting for transfers between devices, send(): return lax.ppermute(value, axis, [(i, (i + step) % n) for i in range(n)])  17.1 us
    pallas_call x3, Pallas kernels, call(): pl.pallas_call(kernel, out_shape=tuple((jax.ShapeDtypeStruct(s, F32) for...  13.5 us
    all_to_all x1, starting transfers between devices, body(): p_all = lax.all_to_all(p_sum, ('yh', 'x', 'yl'), 0, 0)  7.19 us
    all_to_all x1, starting transfers between devices, body(): lax.all_to_all(jnp.broadcast_to(sums.reshape(1, 1, 256), (8, 1, 256)), 'z...  6.84 us
    all_to_all x1, waiting for transfers between devices, body(): lax.all_to_all(jnp.broadcast_to(sums.reshape(1, 1, 256), (8, 1, 256)), 'z...  5.46 us
    transpose x2, other arithmetic, body(): return (residual_next.T, adjoint.T, jnp.sum(sums[0, 128:256]).reshape(1))  2.87 us
  transfers between devices with their start and end apart: 27, of which 9 were waited for; matrix products, arithmetic and copies ran while one was open for 5% of the time, Pallas kernels for 5%

profile of v3, /device:TPU:2, one launch (start us, length us, event | category | flops | bytes accessed | tf_op | source)
XLA Modules:
  0.0 105.6 jit_solution(14369516682386281847)
XLA Ops:
  0.7 1.3 %constant_dynamic-slice_fusion.11 = (bf16[256,64]{1,0:T(8,128)(2,1)S(1)}, bf16[256,64]{1,0:T(8,128)(2,1)S(1)}, bf16[256,64]{1,0:T(8,128)(2,1)S(1)}, bf16[256,64]...) fusion(bf16[256,256]{1,0:T(8,128)(2,1)} %param.8, ...), kind=kLoop, calls=%fused_computation.47 | loop fusion | bytes 524304 | tf_op jit(solution)/shard_map/dynamic_slice | solution.py:123
  2.9 2.3 %collective-permute-start.10 = (bf16[640,256]{1,0:T(8,128)(2,1)S(1)}, bf16[640,256]{1,0:T(8,128)(2,1)S(1)}, u32[]{:S(2)}, u32[]{:S(2)}) collective-permute-start(bf16[640,256]{1,0:T(8,128)(2,1)S(1)} %pad_maximum_fusion.refs_5_.refs_4_.refs_0_), channel_id=1, source_target_pairs={{0,12},{4,0},{8,4},{12,8},{1,13},{5,1},{9,5},{13,9},{2,14},{6,2},{... | collective-permute-start | bytes 983048 | tf_op jit(solution)/shard_map/ppermute | solution.py:22
  5.2 1.5 %collective-permute-start.8 = (bf16[640,256]{1,0:T(8,128)(2,1)S(1)}, bf16[640,256]{1,0:T(8,128)(2,1)S(1)}, u32[]{:S(2)}, u32[]{:S(2)}) collective-permute-start(bf16[640,256]{1,0:T(8,128)(2,1)S(1)} %pad_maximum_fusion.refs_5_.refs_4_.refs_0_), channel_id=1, source_target_pairs={{0,16},{16,0},{1,17},{17,1},{2,18},{18,2},{3,19},{19,3},{4,20},{20... | collective-permute-start | bytes 983048 | tf_op jit(solution)/shard_map/ppermute | solution.py:22
  6.7 1.5 %collective-permute-start.9 = (bf16[640,256]{1,0:T(8,128)(2,1)S(1)}, bf16[640,256]{1,0:T(8,128)(2,1)S(1)}, u32[]{:S(2)}, u32[]{:S(2)}) collective-permute-start(bf16[640,256]{1,0:T(8,128)(2,1)S(1)} %pad_maximum_fusion.refs_5_.refs_4_.refs_0_), channel_id=1, source_target_pairs={{0,4},{4,8},{8,12},{12,0},{1,5},{5,9},{9,13},{13,1},{2,6},{6,10},{... | collective-permute-start | bytes 983048 | tf_op jit(solution)/shard_map/ppermute | solution.py:22
  8.2 2.0 %collective-permute-start = (bf16[512,256]{1,0:T(8,128)(2,1)S(1)}, bf16[512,256]{1,0:T(8,128)(2,1)S(1)}, u32[]{:S(2)}, u32[]{:S(2)}) collective-permute-start(bf16[512,256]{1,0:T(8,128)(2,1)S(1)} %pad_maximum_fusion.1.refs_0_.refs_8_.refs_29_), channel_id=1, source_target_pairs={{0,32},{32,64},{64,96},{96,128},{128,160},{160,192},{192,224},{224... | collective-permute-start | bytes 786440 | tf_op jit(solution)/shard_map/ppermute | solution.py:22
  10.2 4.0 %collective-permute-start.3 = (bf16[512,256]{1,0:T(8,128)(2,1)S(1)}, bf16[512,256]{1,0:T(8,128)(2,1)S(1)}, u32[]{:S(2)}, u32[]{:S(2)}) collective-permute-start(bf16[512,256]{1,0:T(8,128)(2,1)S(1)} %pad_maximum_fusion.1.refs_0_.refs_8_.refs_29_), channel_id=1, source_target_pairs={{0,224},{32,0},{64,32},{96,64},{128,96},{160,128},{192,160},{224,1... | collective-permute-start | bytes 786440 | tf_op jit(solution)/shard_map/ppermute | solution.py:22
  14.2 2.4 %collective-permute-done.9.refs_7_.refs_6_.refs_2_ = bf16[640,256]{1,0:T(8,128)(2,1)S(1)} collective-permute-done((bf16[640,256]{1,0:T(8,128)(2,1)S(1)}, bf16[640,256]{1,0:T(8,128)(2,1)S(1)}, u32[]{:S(2)}, u32[]{:S(2)}) %collective-permute-start.9) | collective-permute-done | bytes 327712 | tf_op jit(solution)/shard_map/ppermute | solution.py:22
  17.1 2.5 %collective-permute-start.12 = (bf16[640,256]{1,0:T(8,128)(2,1)S(1)}, bf16[640,256]{1,0:T(8,128)(2,1)}, u32[]{:S(2)}, u32[]{:S(2)}) collective-permute-start(bf16[640,256]{1,0:T(8,128)(2,1)S(1)} %collective-permute-done.8.refs_6_.refs_5_.refs_1_), channel_id=1, source_target_pairs={{0,12},{4,0},{8,4},{12,8},{1,13},{5,1},{9,5},{13,9},{2,14},{6,2},{... | collective-permute-start | bytes 983048 | tf_op jit(solution)/shard_map/ppermute | solution.py:22
  19.6 1.9 %collective-permute-start.1 = (bf16[512,256]{1,0:T(8,128)(2,1)S(1)}, bf16[512,256]{1,0:T(8,128)(2,1)S(1)}, u32[]{:S(2)}, u32[]{:S(2)}) collective-permute-start(bf16[512,256]{1,0:T(8,128)(2,1)S(1)} %collective-permute-done.refs_1_.refs_9_.refs_17_.refs_23_), channel_id=1, source_target_pairs={{0,32},{32,64},{64,96},{96,128},{128,160},{160,192},{192,224},{224... | collective-permute-start | bytes 786440 | tf_op jit(solution)/shard_map/ppermute | solution.py:22
  21.5 4.0 %collective-permute-start.4 = (bf16[512,256]{1,0:T(8,128)(2,1)S(1)}, bf16[512,256]{1,0:T(8,128)(2,1)S(1)}, u32[]{:S(2)}, u32[]{:S(2)}) collective-permute-start(bf16[512,256]{1,0:T(8,128)(2,1)S(1)} %collective-permute-done.3.refs_2_.refs_10_.refs_18_.refs_24_), channel_id=1, source_target_pairs={{0,224},{32,0},{64,32},{96,64},{128,96},{160,128},{192,160},{224,1... | collective-permute-start | bytes 786440 | tf_op jit(solution)/shard_map/ppermute | solution.py:22
  25.5 4.5 %collective-permute-done.1.refs_3_.refs_11_.refs_19_.refs_25_ = bf16[512,256]{1,0:T(8,128)(2,1)S(1)} collective-permute-done((bf16[512,256]{1,0:T(8,128)(2,1)S(1)}, bf16[512,256]{1,0:T(8,128)(2,1)S(1)}, u32[]{:S(2)}, u32[]{:S(2)}) %collective-permute-start.1) | collective-permute-done | bytes 262176 | tf_op jit(solution)/shard_map/ppermute | solution.py:22
  30.0 3.2 %collective-permute-start.5 = (bf16[512,256]{1,0:T(8,128)(2,1)S(1)}, bf16[512,256]{1,0:T(8,128)(2,1)S(1)}, u32[]{:S(2)}, u32[]{:S(2)}) collective-permute-start(bf16[512,256]{1,0:T(8,128)(2,1)S(1)} %collective-permute-done.4.refs_4_.refs_12_.refs_20_.refs_26_), channel_id=1, source_target_pairs={{0,224},{32,0},{64,32},{96,64},{128,96},{160,128},{192,160},{224,1... | collective-permute-start | bytes 786440 | tf_op jit(solution)/shard_map/ppermute | solution.py:22
  33.2 3.2 %collective-permute-start.14 = (bf16[640,256]{1,0:T(8,128)(2,1)}, bf16[640,256]{1,0:T(8,128)(2,1)}, u32[]{:S(2)}, u32[]{:S(2)}) collective-permute-start(bf16[640,256]{1,0:T(8,128)(2,1)} %collective-permute-done.12.refs_10_.refs_9_.refs_5_), channel_id=1, source_target_pairs={{0,12},{4,0},{8,4},{12,8},{1,13},{5,1},{9,5},{13,9},{2,14},{6,2},{... | collective-permute-start | bytes 983048 | tf_op jit(solution)/shard_map/ppermute | solution.py:22
  36.4 1.1 %collective-permute-done.2.refs_0_.refs_13_.refs_21_.refs_27_ = bf16[512,256]{1,0:T(8,128)(2,1)S(1)} collective-permute-done((bf16[512,256]{1,0:T(8,128)(2,1)S(1)}, bf16[512,256]{1,0:T(8,128)(2,1)S(1)}, u32[]{:S(2)}, u32[]{:S(2)}) %collective-permute-start.2) | collective-permute-done | bytes 262176 | tf_op jit(solution)/shard_map/ppermute | solution.py:22
  38.9 3.2 %collective-permute-start.7 = (bf16[256,256]{1,0:T(8,128)(2,1)}, bf16[256,256]{1,0:T(8,128)(2,1)}, u32[]{:S(2)}, u32[]{:S(2)}) collective-permute-start(bf16[256,256]{1,0:T(8,128)(2,1)} %slice.65), channel_id=1, source_target_pairs={{0,224},{32,0},{64,32},{96,64},{128,96},{160,128},{192,160},{224,1... | collective-permute-start | bytes 393224 | tf_op jit(solution)/shard_map/ppermute | solution.py:22
  42.9 5.5 %tiles_a.1 = (f32[256,2048]{1,0:T(8,128)S(1)}, f32[5,256,256]{2,1,0:T(8,128)S(1)}) custom-call(bf16[512,256]{1,0:T(8,128)(2,1)S(1)} %pad_maximum_fusion.1.refs_0_.refs_8_.refs_29_, bf16[512,256]{1,0:T(8,128)(2,1)S(1)} %collective-permute-done.refs_1_.refs_9_.refs_17_.refs_23_, bf16[512,256]{1,0:T(8,128)(2,1)S(1)} %collective-permute-done.3.refs_2_.refs_10_.refs_18_.refs_24_, ...), custom_call_target="tpu_custom_call" | custom-call | tf_op jit(solution)/shard_map/tiles_a/pallas_call | solution.py:104
  48.5 5.2 %tiles_b.1 = (f32[16,64,256]{2,1,0:T(8,128)S(1)}, f32[16,64,256]{2,1,0:T(8,128)S(1)}, f32[16,64,256]{2,1,0:T(8,128)S(1)}, f32[16,64,256]{2,1,0:T(8,128)}, f32[8,128]{1,0:T(8,128)S(1)}) custom-call(f32[1]{0:T(128)S(6)} %mul.101.w_ref, s32[4]{0:T(128)S(1)} %pad_add_fusion.pos_ref, ...), custom_call_target="tpu_custom_call" | custom-call | tf_op jit(solution)/shard_map/tiles_b/pallas_call | solution.py:104
  54.3 0.9 fusion.1
  55.3 1.0 collective-permute-done.15.theirs
  56.3 2.8 %fold.1 = f32[16,72,256]{2,1,0:T(8,128)} custom-call(s32[4]{0:T(128)S(1)} %pad_add_fusion.pos_ref, f32[16,64,256]{2,1,0:T(8,128)S(1)} %get-tuple-element.35.mine, f32[16,64,256]{2,1,0:T(8,128)S(1)} %collective-permute-done.15.theirs, f32[8,128]{1,0:T(8,128)S(1)} %select_maximum_fusion.base, f32[8,128]{1,0:T(8,128)S(1)} %get-tuple-element.37.grad, ...), custom_call_target="tpu_custom_call" | custom-call | tf_op jit(solution)/shard_map/fold/pallas_call | solution.py:104
  59.2 7.2 %all-to-all-start = ((f32[16,72,256]{2,1,0:T(8,128)}), f32[16,72,256]{2,1,0:T(8,128)S(1)}, u32[]{:S(2)}, u32[]{:S(2)}) async-start(f32[16,72,256]{2,1,0:T(8,128)} %fold.1), calls=%async_computation | async-start | bytes 2359296 | tf_op jit(solution)/shard_map/all_to_all | solution.py:178
  66.7 1.4 %collective-permute-start.18 = (f32[2,64,256]{2,1,0:T(8,128)S(1)}, f32[2,64,256]{2,1,0:T(8,128)S(1)}, u32[]{:S(2)}, u32[]{:S(2)}) collective-permute-start(f32[2,64,256]{2,1,0:T(8,128)S(1)} %reverse_select_fusion.6), channel_id=1, source_target_pairs={{0,224},{32,0},{64,32},{96,64},{128,96},{160,128},{192,160},{224,1... | collective-permute-start | bytes 393224 | tf_op jit(solution)/shard_map/ppermute | solution.py:22
  68.9 4.6 %collective-permute-start.19 = (f32[2,64,256]{2,1,0:T(8,128)S(1)}, f32[2,64,256]{2,1,0:T(8,128)S(1)}, u32[]{:S(2)}, u32[]{:S(2)}) collective-permute-start(f32[2,64,256]{2,1,0:T(8,128)S(1)} %reverse_select_fusion.5), channel_id=1, source_target_pairs={{0,128},{32,160},{64,192},{96,224},{128,0},{160,32},{192,64},{224,... | collective-permute-start | bytes 393224 | tf_op jit(solution)/shard_map/ppermute | solution.py:22
  73.5 1.4 %collective-permute-start.20 = (f32[2,64,256]{2,1,0:T(8,128)S(1)}, f32[2,64,256]{2,1,0:T(8,128)S(1)}, u32[]{:S(2)}, u32[]{:S(2)}) collective-permute-start(f32[2,64,256]{2,1,0:T(8,128)S(1)} %reverse_select_fusion.4), channel_id=1, source_target_pairs={{0,96},{32,128},{64,160},{96,192},{128,224},{160,0},{192,32},{224,... | collective-permute-start | bytes 393224 | tf_op jit(solution)/shard_map/ppermute | solution.py:22
  74.9 4.0 %collective-permute-start.21 = (f32[2,64,256]{2,1,0:T(8,128)S(1)}, f32[2,64,256]{2,1,0:T(8,128)S(1)}, u32[]{:S(2)}, u32[]{:S(2)}) collective-permute-start(f32[2,64,256]{2,1,0:T(8,128)S(1)} %reverse_select_fusion.3), channel_id=1, source_target_pairs={{0,160},{32,192},{64,224},{96,0},{128,32},{160,64},{192,96},{224,1... | collective-permute-start | bytes 393224 | tf_op jit(solution)/shard_map/ppermute | solution.py:22
  79.1 5.3 %collective-permute-done.17 = f32[2,64,256]{2,1,0:T(8,128)S(1)} collective-permute-done((f32[2,64,256]{2,1,0:T(8,128)S(1)}, f32[2,64,256]{2,1,0:T(8,128)S(1)}, u32[]{:S(2)}, u32[]{:S(2)}) %collective-permute-start.17) | collective-permute-done | bytes 131104 | tf_op jit(solution)/shard_map/ppermute | solution.py:22
  85.2 6.8 %all-to-all-start.1 = ((f32[8,1,256]{2,1,0:T(1,128)}), f32[8,1,256]{2,1,0:T(1,128)S(1)}, u32[]{:S(2)}, u32[]{:S(2)}) async-start(f32[8,1,256]{2,1,0:T(1,128)} %broadcast_in_dim.2), calls=%async_computation.1 | async-start | bytes 16384 | tf_op jit(solution)/shard_map/all_to_all | solution.py:195
  92.5 1.8 %collective-permute-done.23 = f32[2,64,256]{2,1,0:T(8,128)S(1)} collective-permute-done((f32[2,64,256]{2,1,0:T(8,128)S(1)}, f32[2,64,256]{2,1,0:T(8,128)S(1)}, u32[]{:S(2)}, u32[]{:S(2)}) %collective-permute-start.23) | collective-permute-done | bytes 131104 | tf_op jit(solution)/shard_map/ppermute | solution.py:22
  94.3 5.5 %all-to-all-done.1 = f32[8,1,256]{2,1,0:T(1,128)S(1)} async-done(((f32[8,1,256]{2,1,0:T(1,128)}), f32[8,1,256]{2,1,0:T(1,128)S(1)}, u32[]{:S(2)}, u32[]{:S(2)}) %all-to-all-start.1) | async-done | bytes 8224 | tf_op jit(solution)/shard_map/all_to_all | solution.py:195
  99.9 1.6 %collective-permute-start.24 = (f32[64,256]{1,0:T(8,128)S(1)}, f32[64,256]{1,0:T(8,128)S(1)}, u32[]{:S(2)}, u32[]{:S(2)}) collective-permute-start(f32[64,256]{1,0:T(8,128)S(1)} %slice_bitcast_fusion), channel_id=1, source_target_pairs={{0,2},{2,0},{1,3},{3,1},{4,6},{6,4},{5,7},{7,5},{8,10},{10,8},{9,1... | collective-permute-start | bytes 196616 | tf_op jit(solution)/shard_map/ppermute | solution.py:22
  101.5 1.5 %fusion.5 = f32[256,64]{0,1:T(8,128)} fusion(f32[64,256]{1,0:T(8,128)S(1)} %slice_reduce_fusion, f32[256,64]{0,1:T(8,128)S(1)} %copy-done.5, f32[]{:T(128)} %bitcast.45, f32[64]{0:T(128)S(1)} %fusion.11, bf16[256,256]{1,0:T(8,128)(2,1)} %copy-done.2), kind=kLoop, calls=%fused_computation.20 | loop fusion | flops 81920 | bytes 229636 | tf_op jit(solution)/shard_map/transpose | solution.py:203
  104.2 1.4 %fusion.8 = f32[256,64]{0,1:T(8,128)} fusion(f32[64,256]{1,0:T(8,128)S(1)} %collective-permute-done.24, f32[2,64,256]{2,1,0:T(8,128)S(1)} %fusion, bf16[256,256]{1,0:T(8,128)(2,1)} %copy-done.3, f32[]{:T(128)} %bitcast.46), kind=kLoop, calls=%fused_computation.25 | loop fusion | flops 65536 | bytes 229380 | tf_op jit(solution)/shard_map/transpose | solution.py:203
  (84 shorter events, 6.9 us)
Async XLA Ops:
  2.8 5.4 %copy-start.2 = (bf16[256,256]{1,0:T(8,128)(2,1)}, bf16[256,256]{1,0:T(8,128)(2,1)S(1)}, u32[]{:S(2)}) copy-start(bf16[256,256]{1,0:T(8,128)(2,1)S(1)} %maximum_bitcast_fusion) | copy-start | bytes 393220
  2.8 35.4 %copy-start.3 = (bf16[256,256]{1,0:T(8,128)(2,1)}, bf16[256,256]{1,0:T(8,128)(2,1)S(1)}, u32[]{:S(2)}) copy-start(bf16[256,256]{1,0:T(8,128)(2,1)S(1)} %maximum_bitcast_fusion.1) | copy-start | bytes 393220
  2.9 11.3 %collective-permute-start.10 = (bf16[640,256]{1,0:T(8,128)(2,1)S(1)}, bf16[640,256]{1,0:T(8,128)(2,1)S(1)}, u32[]{:S(2)}, u32[]{:S(2)}) collective-permute-start(bf16[640,256]{1,0:T(8,128)(2,1)S(1)} %pad_maximum_fusion.refs_5_.refs_4_.refs_0_), channel_id=1, source_target_pairs={{0,12},{4,0},{8,4},{12,8},{1,13},{5,1},{9,5},{13,9},{2,14},{6,2},{... | collective-permute-start | bytes 983048 | tf_op jit(solution)/shard_map/ppermute | solution.py:22
  5.2 9.0 %collective-permute-start.8 = (bf16[640,256]{1,0:T(8,128)(2,1)S(1)}, bf16[640,256]{1,0:T(8,128)(2,1)S(1)}, u32[]{:S(2)}, u32[]{:S(2)}) collective-permute-start(bf16[640,256]{1,0:T(8,128)(2,1)S(1)} %pad_maximum_fusion.refs_5_.refs_4_.refs_0_), channel_id=1, source_target_pairs={{0,16},{16,0},{1,17},{17,1},{2,18},{18,2},{3,19},{19,3},{4,20},{20... | collective-permute-start | bytes 983048 | tf_op jit(solution)/shard_map/ppermute | solution.py:22
  6.7 9.9 %collective-permute-start.9 = (bf16[640,256]{1,0:T(8,128)(2,1)S(1)}, bf16[640,256]{1,0:T(8,128)(2,1)S(1)}, u32[]{:S(2)}, u32[]{:S(2)}) collective-permute-start(bf16[640,256]{1,0:T(8,128)(2,1)S(1)} %pad_maximum_fusion.refs_5_.refs_4_.refs_0_), channel_id=1, source_target_pairs={{0,4},{4,8},{8,12},{12,0},{1,5},{5,9},{9,13},{13,1},{2,6},{6,10},{... | collective-permute-start | bytes 983048 | tf_op jit(solution)/shard_map/ppermute | solution.py:22
  8.2 11.4 %collective-permute-start = (bf16[512,256]{1,0:T(8,128)(2,1)S(1)}, bf16[512,256]{1,0:T(8,128)(2,1)S(1)}, u32[]{:S(2)}, u32[]{:S(2)}) collective-permute-start(bf16[512,256]{1,0:T(8,128)(2,1)S(1)} %pad_maximum_fusion.1.refs_0_.refs_8_.refs_29_), channel_id=1, source_target_pairs={{0,32},{32,64},{64,96},{96,128},{128,160},{160,192},{192,224},{224... | collective-permute-start | bytes 786440 | tf_op jit(solution)/shard_map/ppermute | solution.py:22
  10.2 11.3 %collective-permute-start.3 = (bf16[512,256]{1,0:T(8,128)(2,1)S(1)}, bf16[512,256]{1,0:T(8,128)(2,1)S(1)}, u32[]{:S(2)}, u32[]{:S(2)}) collective-permute-start(bf16[512,256]{1,0:T(8,128)(2,1)S(1)} %pad_maximum_fusion.1.refs_0_.refs_8_.refs_29_), channel_id=1, source_target_pairs={{0,224},{32,0},{64,32},{96,64},{128,96},{160,128},{192,160},{224,1... | collective-permute-start | bytes 786440 | tf_op jit(solution)/shard_map/ppermute | solution.py:22
  16.6 16.6 %collective-permute-start.11 = (bf16[640,256]{1,0:T(8,128)(2,1)S(1)}, bf16[640,256]{1,0:T(8,128)(2,1)S(1)}, u32[]{:S(2)}, u32[]{:S(2)}) collective-permute-start(bf16[640,256]{1,0:T(8,128)(2,1)S(1)} %collective-permute-done.8.refs_6_.refs_5_.refs_1_), channel_id=1, source_target_pairs={{0,4},{4,8},{8,12},{12,0},{1,5},{5,9},{9,13},{13,1},{2,6},{6,10},{... | collective-permute-start | bytes 983048 | tf_op jit(solution)/shard_map/ppermute | solution.py:22
  17.1 16.1 %collective-permute-start.12 = (bf16[640,256]{1,0:T(8,128)(2,1)S(1)}, bf16[640,256]{1,0:T(8,128)(2,1)}, u32[]{:S(2)}, u32[]{:S(2)}) collective-permute-start(bf16[640,256]{1,0:T(8,128)(2,1)S(1)} %collective-permute-done.8.refs_6_.refs_5_.refs_1_), channel_id=1, source_target_pairs={{0,12},{4,0},{8,4},{12,8},{1,13},{5,1},{9,5},{13,9},{2,14},{6,2},{... | collective-permute-start | bytes 983048 | tf_op jit(solution)/shard_map/ppermute | solution.py:22
  19.6 10.3 %collective-permute-start.1 = (bf16[512,256]{1,0:T(8,128)(2,1)S(1)}, bf16[512,256]{1,0:T(8,128)(2,1)S(1)}, u32[]{:S(2)}, u32[]{:S(2)}) collective-permute-start(bf16[512,256]{1,0:T(8,128)(2,1)S(1)} %collective-permute-done.refs_1_.refs_9_.refs_17_.refs_23_), channel_id=1, source_target_pairs={{0,32},{32,64},{64,96},{96,128},{128,160},{160,192},{192,224},{224... | collective-permute-start | bytes 786440 | tf_op jit(solution)/shard_map/ppermute | solution.py:22
  21.5 8.5 %collective-permute-start.4 = (bf16[512,256]{1,0:T(8,128)(2,1)S(1)}, bf16[512,256]{1,0:T(8,128)(2,1)S(1)}, u32[]{:S(2)}, u32[]{:S(2)}) collective-permute-start(bf16[512,256]{1,0:T(8,128)(2,1)S(1)} %collective-permute-done.3.refs_2_.refs_10_.refs_18_.refs_24_), channel_id=1, source_target_pairs={{0,224},{32,0},{64,32},{96,64},{128,96},{160,128},{192,160},{224,1... | collective-permute-start | bytes 786440 | tf_op jit(solution)/shard_map/ppermute | solution.py:22
  30.0 7.6 %collective-permute-start.2 = (bf16[512,256]{1,0:T(8,128)(2,1)S(1)}, bf16[512,256]{1,0:T(8,128)(2,1)S(1)}, u32[]{:S(2)}, u32[]{:S(2)}) collective-permute-start(bf16[512,256]{1,0:T(8,128)(2,1)S(1)} %collective-permute-done.1.refs_3_.refs_11_.refs_19_.refs_25_), channel_id=1, source_target_pairs={{0,32},{32,64},{64,96},{96,128},{128,160},{160,192},{192,224},{224... | collective-permute-start | bytes 786440 | tf_op jit(solution)/shard_map/ppermute | solution.py:22
  30.0 8.2 %collective-permute-start.5 = (bf16[512,256]{1,0:T(8,128)(2,1)S(1)}, bf16[512,256]{1,0:T(8,128)(2,1)S(1)}, u32[]{:S(2)}, u32[]{:S(2)}) collective-permute-start(bf16[512,256]{1,0:T(8,128)(2,1)S(1)} %collective-permute-done.4.refs_4_.refs_12_.refs_20_.refs_26_), channel_id=1, source_target_pairs={{0,224},{32,0},{64,32},{96,64},{128,96},{160,128},{192,160},{224,1... | collective-permute-start | bytes 786440 | tf_op jit(solution)/shard_map/ppermute | solution.py:22
  33.2 9.7 %collective-permute-start.13 = (bf16[640,256]{1,0:T(8,128)(2,1)S(1)}, bf16[640,256]{1,0:T(8,128)(2,1)}, u32[]{:S(2)}, u32[]{:S(2)}) collective-permute-start(bf16[640,256]{1,0:T(8,128)(2,1)S(1)} %collective-permute-done.9.refs_7_.refs_6_.refs_2_), channel_id=1, source_target_pairs={{0,4},{4,8},{8,12},{12,0},{1,5},{5,9},{9,13},{13,1},{2,6},{6,10},{... | collective-permute-start | bytes 983048 | tf_op jit(solution)/shard_map/ppermute | solution.py:22
  33.2 9.7 %collective-permute-start.14 = (bf16[640,256]{1,0:T(8,128)(2,1)}, bf16[640,256]{1,0:T(8,128)(2,1)}, u32[]{:S(2)}, u32[]{:S(2)}) collective-permute-start(bf16[640,256]{1,0:T(8,128)(2,1)} %collective-permute-done.12.refs_10_.refs_9_.refs_5_), channel_id=1, source_target_pairs={{0,12},{4,0},{8,4},{12,8},{1,13},{5,1},{9,5},{13,9},{2,14},{6,2},{... | collective-permute-start | bytes 983048 | tf_op jit(solution)/shard_map/ppermute | solution.py:22
  38.2 10.2 %collective-permute-start.6 = (bf16[256,256]{1,0:T(8,128)(2,1)}, bf16[256,256]{1,0:T(8,128)(2,1)}, u32[]{:S(2)}, u32[]{:S(2)}) collective-permute-start(bf16[256,256]{1,0:T(8,128)(2,1)} %slice.64), channel_id=1, source_target_pairs={{0,32},{32,64},{64,96},{96,128},{128,160},{160,192},{192,224},{224... | collective-permute-start | bytes 393224 | tf_op jit(solution)/shard_map/ppermute | solution.py:22
  38.9 9.6 %collective-permute-start.7 = (bf16[256,256]{1,0:T(8,128)(2,1)}, bf16[256,256]{1,0:T(8,128)(2,1)}, u32[]{:S(2)}, u32[]{:S(2)}) collective-permute-start(bf16[256,256]{1,0:T(8,128)(2,1)} %slice.65), channel_id=1, source_target_pairs={{0,224},{32,0},{64,32},{96,64},{128,96},{160,128},{192,160},{224,1... | collective-permute-start | bytes 393224 | tf_op jit(solution)/shard_map/ppermute | solution.py:22
  48.5 6.7 %copy-start.5 = (f32[256,64]{0,1:T(8,128)S(1)}, f32[256,64]{0,1:T(8,128)}, u32[]{:S(2)}) copy-start(f32[256,64]{0,1:T(8,128)} %param.9) | copy-start | bytes 196612
  53.6 5.4 %copy-start = (f32[16,64,256]{2,1,0:T(8,128)}, f32[16,64,256]{2,1,0:T(8,128)S(1)}, u32[]{:S(2)}) copy-start(f32[16,64,256]{2,1,0:T(8,128)S(1)} %get-tuple-element.40) | copy-start | bytes 3145732
  53.6 2.7 %collective-permute-start.15 = (f32[16,64,256]{2,1,0:T(8,128)S(1)}, f32[16,64,256]{2,1,0:T(8,128)S(1)}, u32[]{:S(2)}, u32[]{:S(2)}) collective-permute-start(f32[16,64,256]{2,1,0:T(8,128)S(1)} %get-tuple-element.36), channel_id=1, source_target_pairs={{0,1},{1,0},{2,3},{3,2},{4,5},{5,4},{6,7},{7,6},{8,9},{9,8},{10,11... | collective-permute-start | bytes 3145736 | tf_op jit(solution)/shard_map/ppermute | solution.py:22
  59.1 7.3 %collective-permute-start.16 = (f32[16,64,256]{2,1,0:T(8,128)}, f32[16,64,256]{2,1,0:T(8,128)S(1)}, u32[]{:S(2)}, u32[]{:S(2)}) collective-permute-start(f32[16,64,256]{2,1,0:T(8,128)} %get-tuple-element.41), channel_id=1, source_target_pairs={{0,1},{1,0},{2,3},{3,2},{4,5},{5,4},{6,7},{7,6},{8,9},{9,8},{10,11... | collective-permute-start | bytes 3145736 | tf_op jit(solution)/shard_map/ppermute | solution.py:22
  59.2 7.2 %copy-start.1 = (f32[16,64,256]{2,1,0:T(8,128)S(1)}, f32[16,64,256]{2,1,0:T(8,128)}, u32[]{:S(2)}) copy-start(f32[16,64,256]{2,1,0:T(8,128)} %copy-done) | copy-start | bytes 3145732
  59.2 25.2 %all-to-all-start = ((f32[16,72,256]{2,1,0:T(8,128)}), f32[16,72,256]{2,1,0:T(8,128)S(1)}, u32[]{:S(2)}, u32[]{:S(2)}) async-start(f32[16,72,256]{2,1,0:T(8,128)} %fold.1), calls=%async_computation | async-start | bytes 2359296 | tf_op jit(solution)/shard_map/all_to_all | solution.py:178
  66.7 12.3 %collective-permute-start.18 = (f32[2,64,256]{2,1,0:T(8,128)S(1)}, f32[2,64,256]{2,1,0:T(8,128)S(1)}, u32[]{:S(2)}, u32[]{:S(2)}) collective-permute-start(f32[2,64,256]{2,1,0:T(8,128)S(1)} %reverse_select_fusion.6), channel_id=1, source_target_pairs={{0,224},{32,0},{64,32},{96,64},{128,96},{160,128},{192,160},{224,1... | collective-permute-start | bytes 393224 | tf_op jit(solution)/shard_map/ppermute | solution.py:22
  68.1 16.3 %collective-permute-start.17 = (f32[2,64,256]{2,1,0:T(8,128)S(1)}, f32[2,64,256]{2,1,0:T(8,128)S(1)}, u32[]{:S(2)}, u32[]{:S(2)}) collective-permute-start(f32[2,64,256]{2,1,0:T(8,128)S(1)} %reverse_select_fusion.7), channel_id=1, source_target_pairs={{0,32},{32,64},{64,96},{96,128},{128,160},{160,192},{192,224},{224... | collective-permute-start | bytes 393224 | tf_op jit(solution)/shard_map/ppermute | solution.py:22
  68.9 23.2 %collective-permute-start.19 = (f32[2,64,256]{2,1,0:T(8,128)S(1)}, f32[2,64,256]{2,1,0:T(8,128)S(1)}, u32[]{:S(2)}, u32[]{:S(2)}) collective-permute-start(f32[2,64,256]{2,1,0:T(8,128)S(1)} %reverse_select_fusion.5), channel_id=1, source_target_pairs={{0,128},{32,160},{64,192},{96,224},{128,0},{160,32},{192,64},{224,... | collective-permute-start | bytes 393224 | tf_op jit(solution)/shard_map/ppermute | solution.py:22
  73.5 19.0 %collective-permute-start.20 = (f32[2,64,256]{2,1,0:T(8,128)S(1)}, f32[2,64,256]{2,1,0:T(8,128)S(1)}, u32[]{:S(2)}, u32[]{:S(2)}) collective-permute-start(f32[2,64,256]{2,1,0:T(8,128)S(1)} %reverse_select_fusion.4), channel_id=1, source_target_pairs={{0,96},{32,128},{64,160},{96,192},{128,224},{160,0},{192,32},{224,... | collective-permute-start | bytes 393224 | tf_op jit(solution)/shard_map/ppermute | solution.py:22
  74.9 17.6 %collective-permute-start.21 = (f32[2,64,256]{2,1,0:T(8,128)S(1)}, f32[2,64,256]{2,1,0:T(8,128)S(1)}, u32[]{:S(2)}, u32[]{:S(2)}) collective-permute-start(f32[2,64,256]{2,1,0:T(8,128)S(1)} %reverse_select_fusion.3), channel_id=1, source_target_pairs={{0,160},{32,192},{64,224},{96,0},{128,32},{160,64},{192,96},{224,1... | collective-permute-start | bytes 393224 | tf_op jit(solution)/shard_map/ppermute | solution.py:22
  79.0 13.5 %collective-permute-start.22 = (f32[2,64,256]{2,1,0:T(8,128)S(1)}, f32[2,64,256]{2,1,0:T(8,128)S(1)}, u32[]{:S(2)}, u32[]{:S(2)}) collective-permute-start(f32[2,64,256]{2,1,0:T(8,128)S(1)} %reverse_select_fusion.2), channel_id=1, source_target_pairs={{0,64},{32,96},{64,128},{96,160},{128,192},{160,224},{192,0},{224,... | collective-permute-start | bytes 393224 | tf_op jit(solution)/shard_map/ppermute | solution.py:22
  84.4 9.9 %collective-permute-start.23 = (f32[2,64,256]{2,1,0:T(8,128)S(1)}, f32[2,64,256]{2,1,0:T(8,128)S(1)}, u32[]{:S(2)}, u32[]{:S(2)}) collective-permute-start(f32[2,64,256]{2,1,0:T(8,128)S(1)} %reverse_select_fusion.1), channel_id=1, source_target_pairs={{0,192},{32,224},{64,0},{96,32},{128,64},{160,96},{192,128},{224,1... | collective-permute-start | bytes 393224 | tf_op jit(solution)/shard_map/ppermute | solution.py:22
  85.2 14.6 %all-to-all-start.1 = ((f32[8,1,256]{2,1,0:T(1,128)}), f32[8,1,256]{2,1,0:T(1,128)S(1)}, u32[]{:S(2)}, u32[]{:S(2)}) async-start(f32[8,1,256]{2,1,0:T(1,128)} %broadcast_in_dim.2), calls=%async_computation.1 | async-start | bytes 16384 | tf_op jit(solution)/shard_map/all_to_all | solution.py:195
  99.9 4.4 %collective-permute-start.24 = (f32[64,256]{1,0:T(8,128)S(1)}, f32[64,256]{1,0:T(8,128)S(1)}, u32[]{:S(2)}, u32[]{:S(2)}) collective-permute-start(f32[64,256]{1,0:T(8,128)S(1)} %slice_bitcast_fusion), channel_id=1, source_target_pairs={{0,2},{2,0},{1,3},{3,1},{4,6},{6,4},{5,7},{7,5},{8,10},{10,8},{9,1... | collective-permute-start | bytes 196616 | tf_op jit(solution)/shard_map/ppermute | solution.py:22
  (1 other events, 2.2 us)
